TPU v7x, 32 devices: a whole 2x2x4 slice. The times are simulated.
32 devices in a mesh: grp: 4 (over x, core), ep: 8 (over z, y).
Axes of the slice: x: 2, y: 2, z: 4, core: 2. Of those that a mesh axis runs over, the one named last changes fastest.
Arguments:
- tokens: bfloat16 [16384, 1536], P(('grp', 'ep')), may hold values from -6 to 6
- segment_ids: int32 [32, 512], P(('grp', 'ep')), may hold values from 0 to 15, never falling along the last dimension, each value on 1 to 256 neighbouring positions
- routes: int32 [16384, 4], P(('grp', 'ep')), may hold values from 0 to 7, all different within a row; in each aligned block of 512 rows (0 to 511, 512 to 1023, ...) at most 384 rows name the same one
- route_gates: float32 [16384, 4], P(('grp', 'ep')), may hold values from 0.125 to 0.5
- attn_gain: float32 [1536], replicated, may hold values from 0.25 to 1.75
- ffn_gain: float32 [1536], replicated, may hold values from 0.25 to 1.75
- query_weight: bfloat16 [1536, 1536], replicated, may hold values from -0.15625 to 0.15625
- key_matrix: bfloat16 [1536, 256], replicated, may hold values from -0.15625 to 0.15625
- value_matrix: bfloat16 [1536, 256], replicated, may hold values from -0.15625 to 0.15625
- output_weight: bfloat16 [1536, 1536], replicated, may hold values from -0.625 to 0.625
- expert_gate: bfloat16 [8, 1536, 768], P('ep'), may hold values from -0.15625 to 0.15625
- expert_up: bfloat16 [8, 1536, 768], P('ep'), may hold values from -0.15625 to 0.15625
- expert_down: bfloat16 [8, 768, 1536], P('ep'), may hold values from -0.21875 to 0.21875
- cotangent: bfloat16 [16384, 1536], P(('grp', 'ep')), may hold values from -6 to 6
Outputs:
- layer_out: bfloat16 [16384, 1536], P(('grp', 'ep'))
- tokens_grad: float32 [16384, 1536], P(('grp', 'ep'))
- query_grad: float32 [1536, 1536], P(('grp', 'ep'))
- key_grad: float32 [1536, 256], P(('grp', 'ep'))
- value_grad: float32 [1536, 256], P(('grp', 'ep'))
- output_grad: float32 [1536, 1536], P(None, ('grp', 'ep'))
- attn_gain_grad: float32 [1536], P(('grp', 'ep'))
- ffn_gain_grad: float32 [1536], P(('grp', 'ep'))
- expert_gate_grad: float32 [8, 1536, 768], P('ep', 'grp')
- expert_up_grad: float32 [8, 1536, 768], P('ep', 'grp')
- expert_down_grad: float32 [8, 768, 1536], P('ep', None, 'grp')
Inputs may be any that keep to these rules, and one draw needn't show every extreme that they name: `routes`: the 4 numbers of a row differ. Among the rows of one device (512 aligned rows) no expert is named more than 384 times, a bound that some block reaches. `segment_ids`: each row never falls; each segment holds 1 to 256 positions, one exactly that many. The positions of a row's largest number are padding.
All inputs are finite; a program needn't handle non-finite values.
Results may differ from a plain program's by a relative error of at most 0.013.
Values may be sent and summed in bfloat16 or wider, within the bound.
A program may use at most 256 MiB of HBM per device.

v0:
```python
import jax
import jax.numpy as jnp
from jax import lax
from jax.sharding import PartitionSpec as P

HEAD_SIZE = 128


EPS = 1e-06
BASE = 10000.0


def apply_rotary(value_rows, cosine_table, sine_table):
    half = value_rows.shape[-1] // 2
    first = value_rows[..., :half]
    second = value_rows[..., half:]
    return jnp.concatenate(
        [first * cosine_table - second * sine_table, second * cosine_table + first * sine_table],
        axis=-1,
    )


def unrotate(value_rows, cosine_table, sine_table):
    half = value_rows.shape[-1] // 2
    first = value_rows[..., :half]
    second = value_rows[..., half:]
    return jnp.concatenate(
        [first * cosine_table + second * sine_table, second * cosine_table - first * sine_table],
        axis=-1,
    )


def glu_value(gate_val, up_val):
    return jax.nn.gelu(gate_val, approximate=True) * up_val


def scores_of(query_rot, key_rot, allowed):
    score = jnp.einsum(
        "tkgd,skd->kgts", query_rot, key_rot, preferred_element_type=jnp.float32
    ) * HEAD_SIZE ** (-0.5)
    return jnp.where(allowed, score, -1e30)


def local(
    tokens,
    segment_ids,
    routes,
    route_gates,
    attn_gain,
    ffn_gain,
    query_weight,
    key_matrix,
    value_matrix,
    output_weight,
    expert_gate,
    expert_up,
    expert_down,
    cotangent,
):
    length_total, width = tokens.shape
    choose = routes.shape[1]
    local_experts = expert_gate.shape[0]
    owners = lax.axis_size("ep")
    experts = owners * local_experts
    capacity = 3 * length_total * choose // (2 * experts)
    query_heads = query_weight.shape[1] // HEAD_SIZE
    key_heads = key_matrix.shape[1] // HEAD_SIZE
    q_per_kv = query_heads // key_heads
    segment = segment_ids[0]
    padding = segment == jnp.max(segment)
    later = jnp.arange(length_total)[:, None] >= jnp.arange(length_total)[None, :]
    diagonal = jnp.arange(length_total)[:, None] == jnp.arange(length_total)[None, :]
    allowed = (
        later
        & (segment[:, None] == segment[None, :])
        & (jnp.logical_not(padding)[None, :] | diagonal)
    )
    position = jnp.arange(length_total, dtype=jnp.float32)
    inverse = BASE ** (-jnp.arange(HEAD_SIZE // 2, dtype=jnp.float32) * 2.0 / HEAD_SIZE)
    angle = position[:, None] * inverse[None, :]
    cosine_table = jnp.cos(angle)[:, None, :]
    sine_table = jnp.sin(angle)[:, None, :]
    tok_float = tokens.astype(jnp.float32)
    scale_first = lax.rsqrt(jnp.mean(tok_float * tok_float, axis=-1, keepdims=True) + EPS)
    normed_first = tok_float * scale_first
    h_first = (normed_first * attn_gain).astype(jnp.bfloat16)
    query_rows = jnp.dot(h_first, query_weight, preferred_element_type=jnp.float32).reshape(
        length_total, query_heads, HEAD_SIZE
    )
    key_rows = jnp.dot(h_first, key_matrix, preferred_element_type=jnp.float32).reshape(
        length_total, key_heads, HEAD_SIZE
    )
    value_low = jnp.dot(h_first, value_matrix, preferred_element_type=jnp.float32).astype(
        jnp.bfloat16
    )
    value_low = value_low.reshape(length_total, key_heads, HEAD_SIZE)
    query_rot = (
        apply_rotary(query_rows, cosine_table, sine_table)
        .astype(jnp.bfloat16)
        .reshape(length_total, key_heads, q_per_kv, HEAD_SIZE)
    )
    key_rot = apply_rotary(key_rows, cosine_table, sine_table).astype(jnp.bfloat16)
    score = scores_of(query_rot, key_rot, allowed)
    row_max = jnp.max(score, axis=-1, keepdims=True)
    expo = jnp.exp(score - row_max)
    row_sum = jnp.sum(expo, axis=-1, keepdims=True)
    log_total = row_max + jnp.log(row_sum)
    probs_low = (expo / row_sum).astype(jnp.bfloat16)
    attended = jnp.einsum(
        "kgts,skd->tkgd", probs_low, value_low, preferred_element_type=jnp.float32
    )
    attended = attended.reshape(length_total, query_heads * HEAD_SIZE).astype(jnp.bfloat16)
    mixed = tok_float + jnp.dot(attended, output_weight, preferred_element_type=jnp.float32)
    scale_second = lax.rsqrt(jnp.mean(mixed * mixed, axis=-1, keepdims=True) + EPS)
    normed_second = mixed * scale_second
    h_second = (normed_second * ffn_gain).astype(jnp.bfloat16)
    flat_routes = routes.reshape(-1)
    assigns = flat_routes.shape[0]
    onehot = (flat_routes[:, None] == jnp.arange(experts, dtype=jnp.int32)[None, :]).astype(
        jnp.int32
    )
    position_in = jnp.sum(jnp.cumsum(onehot, axis=0) * onehot, axis=1) - 1
    slot_index = flat_routes * capacity + position_in
    source = (
        jnp.full((experts * capacity,), assigns, jnp.int32)
        .at[slot_index]
        .set(jnp.arange(assigns, dtype=jnp.int32))
    )
    token_of = source // choose
    h_ext = jnp.concatenate([h_second, jnp.zeros((1, width), jnp.bfloat16)], axis=0)
    send_rows = h_ext[token_of].reshape(owners, local_experts, capacity, width)
    row_entries = lax.all_to_all(send_rows, "ep", split_axis=0, concat_axis=0, tiled=True)
    gate_val = jnp.einsum(
        "secd,edf->secf", row_entries, expert_gate, preferred_element_type=jnp.float32
    )
    up_val = jnp.einsum(
        "secd,edf->secf", row_entries, expert_up, preferred_element_type=jnp.float32
    )
    act = glu_value(gate_val, up_val).astype(jnp.bfloat16)
    result = jnp.einsum("secf,efd->secd", act, expert_down, preferred_element_type=jnp.float32)
    outputs = (result.astype(jnp.bfloat16), row_entries, gate_val, up_val)
    returned = lax.all_to_all(outputs[0], "ep", split_axis=0, concat_axis=0, tiled=True).reshape(
        experts * capacity, width
    )
    picked = returned[slot_index].reshape(length_total, choose, width).astype(jnp.float32)
    layer_out = (mixed + jnp.sum(route_gates[:, :, None] * picked, axis=1)).astype(jnp.bfloat16)
    grad_out = cotangent.astype(jnp.float32)
    slot_grads = (
        (route_gates[:, :, None] * grad_out[:, None, :])
        .astype(jnp.bfloat16)
        .reshape(assigns, width)
    )
    slot_ext = jnp.concatenate([slot_grads, jnp.zeros((1, width), jnp.bfloat16)], axis=0)
    grad_send = slot_ext[source].reshape(owners, local_experts, capacity, width)
    grad_recv = lax.all_to_all(grad_send, "ep", split_axis=0, concat_axis=0, tiled=True)
    recv_rows = outputs[1]
    gate_val = outputs[2]
    up_val = outputs[3]
    act, act_back = jax.vjp(glu_value, gate_val, up_val)
    act_low = act.astype(jnp.bfloat16)
    down_part = jnp.einsum("secf,secd->efd", act_low, grad_recv, preferred_element_type=jnp.float32)
    act_grad = jnp.einsum(
        "secd,efd->secf", grad_recv, expert_down, preferred_element_type=jnp.float32
    )
    gate_grad_val, up_grad_val = act_back(act_grad)
    gate_low = gate_grad_val.astype(jnp.bfloat16)
    up_low = up_grad_val.astype(jnp.bfloat16)
    gate_part = jnp.einsum(
        "secd,secf->edf", recv_rows, gate_low, preferred_element_type=jnp.float32
    )
    up_part = jnp.einsum("secd,secf->edf", recv_rows, up_low, preferred_element_type=jnp.float32)
    rows_grad = jnp.einsum(
        "secf,edf->secd", gate_low, expert_gate, preferred_element_type=jnp.float32
    )
    rows_grad = rows_grad + jnp.einsum(
        "secf,edf->secd", up_low, expert_up, preferred_element_type=jnp.float32
    )
    rows_back = lax.all_to_all(
        rows_grad.astype(jnp.bfloat16), "ep", split_axis=0, concat_axis=0, tiled=True
    )
    rows_back = rows_back.reshape(experts * capacity, width)
    expert_sums = (
        lax.psum_scatter(
            gate_part.astype(jnp.bfloat16), "grp", scatter_dimension=1, tiled=True
        ).astype(jnp.float32),
        lax.psum_scatter(
            up_part.astype(jnp.bfloat16), "grp", scatter_dimension=1, tiled=True
        ).astype(jnp.float32),
        lax.psum_scatter(
            down_part.astype(jnp.bfloat16), "grp", scatter_dimension=2, tiled=True
        ).astype(jnp.float32),
    )
    second_grad = jnp.sum(
        rows_back[slot_index].reshape(length_total, choose, width).astype(jnp.float32), axis=1
    )
    ffn_gain_part = jnp.sum(second_grad * normed_second, axis=0)
    normed_grad = second_grad * ffn_gain
    mixed_grad = grad_out + scale_second * (
        normed_grad - normed_second * jnp.mean(normed_grad * normed_second, axis=-1, keepdims=True)
    )
    mixed_low = mixed_grad.astype(jnp.bfloat16)
    output_part = jnp.einsum("ti,td->id", attended, mixed_low, preferred_element_type=jnp.float32)
    attended_grad = jnp.einsum(
        "td,id->ti", mixed_low, output_weight, preferred_element_type=jnp.float32
    )
    attended_grad = attended_grad.astype(jnp.bfloat16).reshape(
        length_total, key_heads, q_per_kv, HEAD_SIZE
    )
    probs = jnp.exp(scores_of(query_rot, key_rot, allowed) - log_total)
    probs_again = probs.astype(jnp.bfloat16)
    value_part_grad = jnp.einsum(
        "kgts,tkgd->skd", probs_again, attended_grad, preferred_element_type=jnp.float32
    )
    prob_grad = jnp.einsum(
        "tkgd,skd->kgts", attended_grad, value_low, preferred_element_type=jnp.float32
    )
    inner = jnp.sum(probs * prob_grad, axis=-1, keepdims=True)
    score_grad = (probs * (prob_grad - inner)).astype(jnp.bfloat16)
    qrot_grad = jnp.einsum(
        "kgts,skd->tkgd", score_grad, key_rot, preferred_element_type=jnp.float32
    ) * HEAD_SIZE ** (-0.5)
    krot_grad = jnp.einsum(
        "kgts,tkgd->skd", score_grad, query_rot, preferred_element_type=jnp.float32
    ) * HEAD_SIZE ** (-0.5)
    query_grad_low = unrotate(
        qrot_grad.reshape(length_total, query_heads, HEAD_SIZE), cosine_table, sine_table
    )
    query_grad_low = query_grad_low.astype(jnp.bfloat16).reshape(
        length_total, query_heads * HEAD_SIZE
    )
    key_grad_low = (
        unrotate(krot_grad, cosine_table, sine_table)
        .astype(jnp.bfloat16)
        .reshape(length_total, key_heads * HEAD_SIZE)
    )
    value_grad_low = value_part_grad.astype(jnp.bfloat16).reshape(
        length_total, key_heads * HEAD_SIZE
    )
    query_part = jnp.einsum(
        "td,ti->di", h_first, query_grad_low, preferred_element_type=jnp.float32
    )
    key_part = jnp.einsum("td,ti->di", h_first, key_grad_low, preferred_element_type=jnp.float32)
    value_part = jnp.einsum(
        "td,ti->di", h_first, value_grad_low, preferred_element_type=jnp.float32
    )
    first_grad = jnp.einsum(
        "ti,di->td", query_grad_low, query_weight, preferred_element_type=jnp.float32
    )
    first_grad = first_grad + jnp.einsum(
        "ti,di->td", key_grad_low, key_matrix, preferred_element_type=jnp.float32
    )
    first_grad = first_grad + jnp.einsum(
        "ti,di->td", value_grad_low, value_matrix, preferred_element_type=jnp.float32
    )
    attn_gain_part = jnp.sum(first_grad * normed_first, axis=0)
    normed_first_grad = first_grad * attn_gain
    tokens_grad = mixed_grad + scale_first * (
        normed_first_grad
        - normed_first * jnp.mean(normed_first_grad * normed_first, axis=-1, keepdims=True)
    )
    shared = (
        lax.psum_scatter(query_part, ("grp", "ep"), scatter_dimension=0, tiled=True),
        lax.psum_scatter(key_part, ("grp", "ep"), scatter_dimension=0, tiled=True),
        lax.psum_scatter(value_part, ("grp", "ep"), scatter_dimension=0, tiled=True),
        lax.psum_scatter(output_part, ("grp", "ep"), scatter_dimension=1, tiled=True),
        lax.psum_scatter(attn_gain_part, ("grp", "ep"), scatter_dimension=0, tiled=True),
        lax.psum_scatter(ffn_gain_part, ("grp", "ep"), scatter_dimension=0, tiled=True),
    )
    return (
        layer_out,
        tokens_grad,
        shared[0],
        shared[1],
        shared[2],
        shared[3],
        shared[4],
        shared[5],
        expert_sums[0],
        expert_sums[1],
        expert_sums[2],
    )


def solution(mesh):
    in_specs = (
        P(("grp", "ep"), None),
        P(("grp", "ep"), None),
        P(("grp", "ep"), None),
        P(("grp", "ep"), None),
        P(),
        P(),
        P(),
        P(),
        P(),
        P(),
        P("ep", None, None),
        P("ep", None, None),
        P("ep", None, None),
        P(("grp", "ep"), None),
    )
    out_specs = (
        P(("grp", "ep"), None),
        P(("grp", "ep"), None),
        P(("grp", "ep"), None),
        P(("grp", "ep"), None),
        P(("grp", "ep"), None),
        P(None, ("grp", "ep")),
        P(("grp", "ep")),
        P(("grp", "ep")),
        P("ep", "grp", None),
        P("ep", "grp", None),
        P("ep", None, "grp"),
    )
    return jax.shard_map(local, mesh=mesh, in_specs=in_specs, out_specs=out_specs, check_vma=False)
```

profile of v0, /device:TPU:0, one launch (start us, length us, event | category | flops | bytes accessed | tf_op | source)
XLA Modules:
  0.0 1569.2 jit_solution(8342260426700957017)
XLA Ops:
  14.1 8.1 scatter_custom_fusion
  29.3 14.9 mul.506
  58.0 22.9 %gather_fusion.2 = bf16[3072,1536]{1,0:T(8,128)(2,1)} fusion(bf16[2049,1536]{1,0:T(8,128)(2,1)} %concatenate.32, s32[3072]{0:T(1024)S(1)} %get-tuple-element.32), kind=kCustom, calls=%fused_computation.2 | custom fusion | bytes 18886656 | tf_op jit(solution)/shard_map/gather | solution.py:154
  135.1 20.9 %gather_fusion = bf16[3072,1536]{1,0:T(8,128)(2,1)} fusion(bf16[513,1536]{1,0:T(8,128)(2,1)} %concatenate.31, s32[3072]{0:T(1024)S(1)} %get-tuple-element.33), kind=kCustom, calls=%fused_computation | custom fusion | bytes 18886656 | tf_op jit(solution)/shard_map/gather | solution.py:131
  156.1 137.9 %all-to-all-done.2 = bf16[8,1,384,1536]{3,2,1,0:T(8,128)(2,1)} async-done(((bf16[8,1,384,1536]{3,2,1,0:T(8,128)(2,1)}), bf16[8,1,384,1536]{3,2,1,0:T(8,128)(2,1)}, u32[]{:S(2)}, u32[]{:S(2)}) %all-to-all-start.2) | async-done | bytes 9437216 | tf_op jit(solution)/shard_map/all_to_all | solution.py:155
  299.4 13.0 fusion.17
  312.4 191.7 %all-to-all-done = bf16[8,1,384,1536]{3,2,1,0:T(8,128)(2,1)} async-done(((bf16[8,1,384,1536]{3,2,1,0:T(8,128)(2,1)}), bf16[8,1,384,1536]{3,2,1,0:T(8,128)(2,1)}, u32[]{:S(2)}, u32[]{:S(2)}) %all-to-all-start) | async-done | bytes 9437216 | tf_op jit(solution)/shard_map/all_to_all | solution.py:132
  504.1 13.0 fusion.25
  517.1 22.6 %fusion.38 = (bf16[8,384,768]{2,1,0:T(8,128)(2,1)}, bf16[8,1,384,768]{3,2,0,1:T(8,128)(2,1)}, bf16[8,384,768]{2,1,0:T(8,128)(2,1)}) fusion(f32[8,384,768]{2,1,0:T(8,128)} %fusion.17, f32[8,384,768]{2,1,0:T(8,128)} %fusion.25, bf16[1,1536,768]{2,1,0:T(8,128)(2,1)S(1)} %copy-done, bf16[8,1,384,1536]{3,2,1,0:T(8,128)(2,1)} %all-to-all-done), kind=kOutput, calls=%fused_computation.62 | convolution fusion | flops 7309099008 | bytes 44826624 | tf_op jit(solution)/shard_map/secd,edf->secf/dot_general | solution.py:133
  539.7 12.1 convert_bitcast_fusion
  556.9 13.2 fusion.40
  570.1 15.9 %fusion.12 = bf16[8,1,384,1536]{3,2,1,0:T(8,128)(2,1)} fusion(f32[8,384,1536]{2,1,0:T(8,128)} %fusion.40, bf16[8,384,768]{2,1,0:T(8,128)(2,1)} %get-tuple-element.17, bf16[1,1536,768]{2,1,0:T(8,128)(2,1)S(1)} %copy-done.59), kind=kOutput, calls=%fused_computation.28 | convolution fusion | flops 7257194496 | bytes 35389440 | tf_op jit(solution)/shard_map/secf,edf->secd/dot_general | solution.py:175
  586.0 175.2 %all-to-all-done.1 = bf16[8,1,384,1536]{3,2,1,0:T(8,128)(2,1)} async-done(((bf16[8,1,384,1536]{3,2,1,0:T(8,128)(2,1)}), bf16[8,1,384,1536]{3,2,1,0:T(8,128)(2,1)}, u32[]{:S(2)}, u32[]{:S(2)}) %all-to-all-start.1) | async-done | bytes 9437216 | tf_op jit(solution)/shard_map/all_to_all | solution.py:142
  766.3 11.6 fusion.66
  778.0 8.4 copy.122
  790.6 12.9 fusion.63
  803.7 12.7 fusion.58
  816.4 18.6 %gather_fusion.1 = bf16[2048,1536]{1,0:T(8,128)(2,1)} fusion(bf16[3072,1536]{1,0:T(8,128)(2,1)} %bitcast.38, s32[2048]{0:T(1024)S(1)} %broadcast_clamp_fusion), kind=kCustom, calls=%fused_computation.1 | custom fusion | bytes 12591104 | tf_op jit(solution)/shard_map/gather | solution.py:145
  835.0 12.3 reshape.273
  847.4 123.6 %all-to-all-done.3 = bf16[8,1,384,1536]{3,2,1,0:T(8,128)(2,1)} async-done(((bf16[8,1,384,1536]{3,2,1,0:T(8,128)(2,1)}), bf16[8,1,384,1536]{3,2,1,0:T(8,128)(2,1)}, u32[]{:S(2)}, u32[]{:S(2)}) %all-to-all-start.3) | async-done | bytes 9437216 | tf_op jit(solution)/shard_map/all_to_all | solution.py:178
  971.0 18.1 %gather_fusion.3 = bf16[2048,1536]{1,0:T(8,128)(2,1)} fusion(bf16[3072,1536]{1,0:T(8,128)(2,1)} %bitcast.55, s32[2048]{0:T(1024)S(1)} %broadcast_clamp_fusion), kind=kCustom, calls=%fused_computation.3 | custom fusion | bytes 12591104 | tf_op jit(solution)/shard_map/gather | solution.py:194
  989.1 12.2 reshape.274
  1001.3 12.6 reduce_sum.104
  1017.8 32.6 %multiply_reduce_fusion = f32[512,1536]{1,0:T(8,128)S(1)} fusion(f32[512,4,1536]{2,1,0:T(4,128)} %reshape.273, f32[512,4]{1,0:T(8,128)S(1)} %copy-done.23), kind=kLoop, calls=%fused_computation.16 | loop fusion | flops 5505024 | bytes 15736832 | tf_op jit(solution)/shard_map/reduce_sum | solution.py:146
  1058.6 8.5 fusion.81
  1069.7 10.0 fusion
  1079.8 10.8 fusion.2
  1096.8 8.7 fusion.87
  1136.3 38.5 %all-reduce.4 = (f32[1536]{0:T(1024)S(1)}, f32[1536]{0:T(1024)S(1)}) all-reduce(f32[1536]{0:T(1024)S(1)} %get-tuple-element.13, f32[1536]{0:T(1024)S(1)} %get-tuple-element.11), channel_id=6, replica_groups=mesh['grp'=4,'ep'=8] {'grp','ep'}, use_global_device_ids=true, to_apply=%region_19.20.clone | all-reduce | flops 3072 | bytes 24576
  1181.9 97.0 %reduce-scatter.12.cloned.1.call-done = f32[48,256]{1,0:T(8,128)} async-done(((f32[1536,256]{1,0:T(8,128)}), f32[48,256]{1,0:T(8,128)}) %reduce-scatter.12.cloned.1.call-update) | async-done | bytes 49168 | tf_op jit(solution)/shard_map/reduce_scatter | solution.py:263
  1278.8 141.8 %reduce-scatter.16.cloned.1.call-done = f32[1536,48]{0,1:T(8,128)} async-done(((f32[1536,1536]{0,1:T(8,128)}), f32[1536,48]{0,1:T(8,128)}) %reduce-scatter.16.cloned.1.call-update) | async-done | bytes 294928 | tf_op jit(solution)/shard_map/reduce_scatter | solution.py:265
  1420.7 141.3 %reduce-scatter.10.cloned.1.call-done = f32[48,1536]{1,0:T(8,128)} async-done(((f32[1536,1536]{1,0:T(8,128)}), f32[48,1536]{1,0:T(8,128)}) %reduce-scatter.10.cloned.1.call-update) | async-done | bytes 294928 | tf_op jit(solution)/shard_map/reduce_scatter | solution.py:262
  (224 shorter events, 160.0 us)
Async XLA Ops:
  7.2 509.9 %copy-start = (bf16[1,1536,768]{2,1,0:T(8,128)(2,1)S(1)}, bf16[1,1536,768]{2,1,0:T(8,128)(2,1)}, u32[]{:S(2)}) copy-start(bf16[1,1536,768]{2,1,0:T(8,128)(2,1)} %param.24) | copy-start | bytes 7077892
  10.4 18.9 %copy-start.22 = (f32[512,4]{1,0:T(8,128)}, f32[512,4]{1,0:T(8,128)S(1)}, u32[]{:S(2)}) copy-start(f32[512,4]{1,0:T(8,128)S(1)} %copy.79) | copy-start | bytes 24580
  80.9 213.1 %all-to-all-start.2 = ((bf16[8,1,384,1536]{3,2,1,0:T(8,128)(2,1)}), bf16[8,1,384,1536]{3,2,1,0:T(8,128)(2,1)}, u32[]{:S(2)}, u32[]{:S(2)}) async-start(bf16[8,1,384,1536]{3,2,1,0:T(8,128)(2,1)} %bitcast.282), calls=%async_computation.2 | async-start | bytes 18874368 | tf_op jit(solution)/shard_map/all_to_all | solution.py:155
  89.3 21.9 %copy-start.18 = (f32[512,64]{1,0:T(8,128)}, f32[512,64]{1,0:T(8,128)S(1)}, u32[]{:S(2)}) copy-start(f32[512,64]{1,0:T(8,128)S(1)} %get-tuple-element.34) | copy-start | bytes 393220
  89.4 21.9 %copy-start.20 = (f32[512,64]{1,0:T(8,128)}, f32[512,64]{1,0:T(8,128)S(1)}, u32[]{:S(2)}) copy-start(f32[512,64]{1,0:T(8,128)S(1)} %get-tuple-element.35) | copy-start | bytes 393220
  89.5 13.3 copy-start.30
  89.6 13.2 copy-start.32
  91.5 21.3 %copy-start.55 = (f32[512]{0:T(512)}, f32[512]{0:T(512)S(1)}, u32[]{:S(2)}) copy-start(f32[512]{0:T(512)S(1)} %add_rsqrt_fusion.1) | copy-start | bytes 6148
  294.0 210.1 %all-to-all-start = ((bf16[8,1,384,1536]{3,2,1,0:T(8,128)(2,1)}), bf16[8,1,384,1536]{3,2,1,0:T(8,128)(2,1)}, u32[]{:S(2)}, u32[]{:S(2)}) async-start(bf16[8,1,384,1536]{3,2,1,0:T(8,128)(2,1)} %bitcast.283), calls=%async_computation | async-start | bytes 18874368 | tf_op jit(solution)/shard_map/all_to_all | solution.py:132
  517.1 22.6 %copy-start.58 = (bf16[1,768,1536]{2,1,0:T(8,128)(2,1)S(1)}, bf16[1,768,1536]{2,1,0:T(8,128)(2,1)}, u32[]{:S(2)}) copy-start(bf16[1,768,1536]{2,1,0:T(8,128)(2,1)} %param.26) | copy-start | bytes 7077892
  551.8 209.4 %all-to-all-start.1 = ((bf16[8,1,384,1536]{3,2,1,0:T(8,128)(2,1)}), bf16[8,1,384,1536]{3,2,1,0:T(8,128)(2,1)}, u32[]{:S(2)}, u32[]{:S(2)}) async-start(bf16[8,1,384,1536]{3,2,1,0:T(8,128)(2,1)} %convert_bitcast_fusion), calls=%async_computation.1 | async-start | bytes 18874368 | tf_op jit(solution)/shard_map/all_to_all | solution.py:142
  556.9 13.2 copy-start.59
  761.2 209.7 %all-to-all-start.3 = ((bf16[8,1,384,1536]{3,2,1,0:T(8,128)(2,1)}), bf16[8,1,384,1536]{3,2,1,0:T(8,128)(2,1)}, u32[]{:S(2)}, u32[]{:S(2)}) async-start(bf16[8,1,384,1536]{3,2,1,0:T(8,128)(2,1)} %fusion.12), calls=%async_computation.3 | async-start | bytes 18874368 | tf_op jit(solution)/shard_map/all_to_all | solution.py:178
  766.3 351.9 %reduce-scatter.22.cloned.1.call-start = ((), (), s32[]{:S(2)}) async-start(), calls=%async_computation.17 | async-start | bytes 2949120
  790.5 13.1 copy-start.52
  790.6 13.1 copy-start.39
  790.6 13.1 copy-start.45
  790.6 332.1 %reduce-scatter.20.cloned.1.call-start = ((), (), s32[]{:S(2)}) async-start(), calls=%async_computation.16 | async-start | bytes 2949120 | tf_op jit(solution)/shard_map/reduce_scatter | solution.py:186
  803.5 321.3 %reduce-scatter.18.cloned.1.call-start = ((), (), s32[]{:S(2)}) async-start(), calls=%async_computation.15 | async-start | bytes 2949120 | tf_op jit(solution)/shard_map/reduce_scatter | solution.py:183
  816.4 365.5 %reduce-scatter.14.cloned.1.call-start = ((), (), s32[]{:S(2)}) async-start(), calls=%async_computation.13 | async-start | bytes 1622016 | tf_op jit(solution)/shard_map/reduce_scatter | solution.py:264
  1001.3 12.6 copy-start.47
  1001.3 12.6 copy-start.49
  1013.9 40.4 %slice-start = ((s8[4718592]{0:T(1024)(128)(4,1)}), s8[4194304]{0:T(1024)(128)(4,1)S(1)}, s32[]{:S(2)}) async-start(s8[4718592]{0:T(1024)(128)(4,1)} %bitcast.310), calls=%async_computation.18 | async-start | bytes 8388608
  1017.7 32.6 %copy-start.5 = (f32[512,1536]{1,0:T(8,128)S(1)}, f32[512,1536]{1,0:T(8,128)}, u32[]{:S(2)}) copy-start(f32[512,1536]{1,0:T(8,128)} %copy-done.4) | copy-start | bytes 9437188
  1017.7 32.6 %copy-start.6 = (f32[512,1536]{1,0:T(8,128)S(1)}, f32[512,1536]{1,0:T(8,128)}, u32[]{:S(2)}) copy-start(f32[512,1536]{1,0:T(8,128)} %reduce_sum.104) | copy-start | bytes 9437188
  1017.7 32.6 %copy-start.17 = (bf16[512,1536]{1,0:T(8,128)(2,1)S(1)}, bf16[512,1536]{1,0:T(8,128)(2,1)}, u32[]{:S(2)}) copy-start(bf16[512,1536]{1,0:T(8,128)(2,1)} %param.27) | copy-start | bytes 4718596
  1017.7 36.6 %slice-start.1 = ((s8[4718592]{0:T(1024)(128)(4,1)}), s8[524288]{0:T(1024)(128)(4,1)S(1)}, s32[]{:S(2)}) async-start(s8[4718592]{0:T(1024)(128)(4,1)} %bitcast.310), calls=%async_computation.19 | async-start | bytes 1048576
  1079.7 199.1 %reduce-scatter.12.cloned.1.call-start = ((), (), s32[]{:S(2)}) async-start(), calls=%async_computation.12 | async-start | bytes 1622016 | tf_op jit(solution)/shard_map/reduce_scatter | solution.py:263
  1093.9 11.6 copy-start.34
  1096.7 323.9 %reduce-scatter.16.cloned.1.call-start = ((), (), s32[]{:S(2)}) async-start(), calls=%async_computation.14 | async-start | bytes 9732096 | tf_op jit(solution)/shard_map/reduce_scatter | solution.py:265
  1105.5 456.4 %reduce-scatter.10.cloned.1.call-start = ((), (), s32[]{:S(2)}) async-start(), calls=%async_computation.11 | async-start | bytes 9732096 | tf_op jit(solution)/shard_map/reduce_scatter | solution.py:262
  1176.0 386.0 %copy-start.1 = (bf16[1,1536,768]{2,1,0:T(8,128)(2,1)S(1)}, bf16[1,1536,768]{2,1,0:T(8,128)(2,1)}, u32[]{:S(2)}) copy-start(bf16[1,1536,768]{2,1,0:T(8,128)(2,1)} %param.24) | copy-start | bytes 7077892
  (41 other events, 184.2 us)
Sparse Core Ops, SparseCore 0:
  790.7 34.3 reduce-scatter.21
  827.7 33.0 reduce-scatter.19
  863.3 33.0 reduce-scatter.17
  1079.9 96.3 reduce-scatter.13
  1182.8 95.9 reduce-scatter.11
  1286.2 134.4 reduce-scatter.15
  1427.1 134.7 reduce-scatter.9
where the time goes:
time: 1580 us; the launch traced here: 1570 us
  waiting for transfers between devices  1010 us (64%)
  matrix products  204 us (13%)
  local copies, waits for them, and re-layouts  183 us (12%)
  other arithmetic  96.7 us (6%)
  blocking collectives  38.5 us (2%)
  starting transfers between devices  23.3 us (1%)
    all_to_all x1, waiting for transfers between devices, local(): lax.all_to_all(send_rows, 'ep', split_axis=0, concat_axis=0, tiled=True)  192 us
    all_to_all x1, waiting for transfers between devices, local(): lax.all_to_all(outputs[0], 'ep', split_axis=0, concat_axis=0, tiled=True)  175 us
    reduce_scatter x1, waiting for transfers between devices, local(): lax.psum_scatter(output_part, ('grp', 'ep'), scatter_dimension=1, tiled=T...  142 us
    reduce_scatter x1, waiting for transfers between devices, local(): lax.psum_scatter(query_part, ('grp', 'ep'), scatter_dimension=0, tiled=True)  141 us
    all_to_all x1, waiting for transfers between devices, local(): lax.all_to_all(grad_send, 'ep', split_axis=0, concat_axis=0, tiled=True)  138 us
    all_to_all x1, waiting for transfers between devices, local(): lax.all_to_all(rows_grad.astype(jnp.bfloat16), 'ep', split_axis=0, concat...  124 us
    reduce_scatter x1, waiting for transfers between devices, local(): lax.psum_scatter(key_part, ('grp', 'ep'), scatter_dimension=0, tiled=True)  97 us
    unnamed x1, blocking collectives  38.5 us
  transfers between devices with their start and end apart: 11, of which 7 were waited for; matrix products, arithmetic and copies ran while one was open for 22% of the time, Pallas kernels for 0%

commit v1 on v0

--- a/solution.py
+++ b/solution.py
@@ -41,7 +41,7 @@
     return jnp.where(allowed, score, -1e30)
 
 
-def local(
+def local_routed(
     tokens,
     segment_ids,
     routes,
@@ -281,6 +281,276 @@
     )
 
 
+def local_dense(
+    tokens,
+    segment_ids,
+    routes,
+    route_gates,
+    attn_gain,
+    ffn_gain,
+    query_weight,
+    key_matrix,
+    value_matrix,
+    output_weight,
+    expert_gate,
+    expert_up,
+    expert_down,
+    cotangent,
+):
+    f32, bf16 = jnp.float32, jnp.bfloat16
+    length_total, width = tokens.shape
+    owners = lax.axis_size("ep")
+    experts = owners
+    bit_y, bit_z, bit_far, bit_core, bit_x = 1, 2, owners // 2, owners, 2 * owners
+    names = ("grp", "ep")
+    count = lax.axis_size("grp") * owners
+    me = lax.axis_index("grp") * owners + lax.axis_index("ep")
+    core = (me // bit_core) % 2
+    side = (me // bit_x) % 2
+    on_core1 = core == 1
+
+    def swap(value, mask):
+        return lax.ppermute(value, names, [(i, i ^ mask) for i in range(count)])
+
+    def swap_mixed(value, mask0, mask1):
+        return lax.ppermute(
+            value, names, [(i, i ^ (mask1 if i & bit_core else mask0)) for i in range(count)]
+        )
+
+    def swap_core1(value, mask):
+        return lax.ppermute(value, names, [(i, i ^ mask) for i in range(count) if i & bit_core])
+
+    def gather_group(chunk):
+        from_y = swap(chunk, bit_y)
+        from_z = swap(chunk, bit_z)
+        far = swap_mixed(jnp.where(on_core1, from_y, from_z), bit_y, bit_z)
+        mine = [chunk, from_y, from_z, far]
+        return mine + [swap(part, bit_core) for part in mine]
+
+    def reduce_group(parts):
+        own, to_y, to_z, far = [
+            parts[i].astype(f32) + swap(parts[4 + i], bit_core).astype(f32) for i in range(4)
+        ]
+        passed = swap_mixed(far.astype(bf16), bit_y, bit_z).astype(f32)
+        to_y = to_y + jnp.where(on_core1, passed, 0.0)
+        to_z = to_z + jnp.where(on_core1, 0.0, passed)
+        return own + swap(to_y.astype(bf16), bit_y).astype(f32) + swap(
+            to_z.astype(bf16), bit_z
+        ).astype(f32)
+
+    def fetch(weight):
+        rows = weight.shape[0] // 2
+        half = lax.dynamic_slice_in_dim(weight, side * rows, rows, 0)
+        here = swap_core1(half, bit_far)
+        there = swap_core1(here, bit_x)
+        low = jnp.where(side == 0, here, there)
+        high = jnp.where(side == 0, there, here)
+        return jnp.where(on_core1, jnp.concatenate([low, high], axis=0), weight)
+
+    def give(grad, dim):
+        size = grad.shape[dim] // 2
+        sent = lax.dynamic_slice_in_dim(grad, (1 - side) * size, size, dim).astype(bf16)
+        kept = lax.dynamic_slice_in_dim(grad, side * size, size, dim)
+        half = kept + swap(sent, bit_x).astype(f32)
+        foreign = swap_core1(half.astype(bf16), bit_far).astype(f32)
+        base = jnp.where(on_core1, foreign, half)
+        size = size // 2
+        sent = lax.dynamic_slice_in_dim(base, (1 - core) * size, size, dim).astype(bf16)
+        kept = lax.dynamic_slice_in_dim(base, core * size, size, dim)
+        return kept + swap(sent, bit_core).astype(f32)
+
+    def reduce_all(value):
+        order = [bit_core, bit_x, bit_y, bit_z, bit_far]
+        bits = [bit_x, bit_core, bit_far, bit_z, bit_y]
+        rows, columns = value.shape
+        block = value.reshape((2,) * 5 + (rows // count, columns))
+        for mask in order:
+            axis = bits.index(mask)
+            mine = (me // mask) % 2
+            sent = lax.dynamic_slice_in_dim(block, 1 - mine, 1, axis)
+            kept = lax.dynamic_slice_in_dim(block, mine, 1, axis)
+            block = kept.astype(f32) + swap(sent.astype(bf16), mask).astype(f32)
+        return block.reshape(rows // count, columns)
+
+    cotangent_parts = gather_group(cotangent)
+    weight_gate = fetch(expert_gate[0])
+    weight_up = fetch(expert_up[0])
+    weight_down = fetch(expert_down[0])
+    table = jnp.sum(
+        jnp.where(
+            routes[:, :, None] == jnp.arange(experts, dtype=jnp.int32)[None, None, :],
+            route_gates[:, :, None],
+            0.0,
+        ),
+        axis=1,
+    )
+    tables = jnp.stack(gather_group(table.T))
+    hosted = lax.axis_index("ep") ^ (bit_far * core)
+    gate_column = lax.dynamic_index_in_dim(tables, hosted, 1, keepdims=False).reshape(-1)[:, None]
+
+    query_heads = query_weight.shape[1] // HEAD_SIZE
+    key_heads = key_matrix.shape[1] // HEAD_SIZE
+    q_per_kv = query_heads // key_heads
+    segment = segment_ids[0]
+    padding = segment == jnp.max(segment)
+    later = jnp.arange(length_total)[:, None] >= jnp.arange(length_total)[None, :]
+    diagonal = jnp.arange(length_total)[:, None] == jnp.arange(length_total)[None, :]
+    allowed = (
+        later
+        & (segment[:, None] == segment[None, :])
+        & (jnp.logical_not(padding)[None, :] | diagonal)
+    )
+    position = jnp.arange(length_total, dtype=jnp.float32)
+    inverse = BASE ** (-jnp.arange(HEAD_SIZE // 2, dtype=jnp.float32) * 2.0 / HEAD_SIZE)
+    angle = position[:, None] * inverse[None, :]
+    cosine_table = jnp.cos(angle)[:, None, :]
+    sine_table = jnp.sin(angle)[:, None, :]
+    tok_float = tokens.astype(jnp.float32)
+    scale_first = lax.rsqrt(jnp.mean(tok_float * tok_float, axis=-1, keepdims=True) + EPS)
+    normed_first = tok_float * scale_first
+    h_first = (normed_first * attn_gain).astype(jnp.bfloat16)
+    query_rows = jnp.dot(h_first, query_weight, preferred_element_type=jnp.float32).reshape(
+        length_total, query_heads, HEAD_SIZE
+    )
+    key_rows = jnp.dot(h_first, key_matrix, preferred_element_type=jnp.float32).reshape(
+        length_total, key_heads, HEAD_SIZE
+    )
+    value_low = jnp.dot(h_first, value_matrix, preferred_element_type=jnp.float32).astype(
+        jnp.bfloat16
+    )
+    value_low = value_low.reshape(length_total, key_heads, HEAD_SIZE)
+    query_rot = (
+        apply_rotary(query_rows, cosine_table, sine_table)
+        .astype(jnp.bfloat16)
+        .reshape(length_total, key_heads, q_per_kv, HEAD_SIZE)
+    )
+    key_rot = apply_rotary(key_rows, cosine_table, sine_table).astype(jnp.bfloat16)
+    score = scores_of(query_rot, key_rot, allowed)
+    row_max = jnp.max(score, axis=-1, keepdims=True)
+    expo = jnp.exp(score - row_max)
+    row_sum = jnp.sum(expo, axis=-1, keepdims=True)
+    log_total = row_max + jnp.log(row_sum)
+    probs_low = (expo / row_sum).astype(jnp.bfloat16)
+    attended = jnp.einsum(
+        "kgts,skd->tkgd", probs_low, value_low, preferred_element_type=jnp.float32
+    )
+    attended = attended.reshape(length_total, query_heads * HEAD_SIZE).astype(jnp.bfloat16)
+    mixed = tok_float + jnp.dot(attended, output_weight, preferred_element_type=jnp.float32)
+    scale_second = lax.rsqrt(jnp.mean(mixed * mixed, axis=-1, keepdims=True) + EPS)
+    normed_second = mixed * scale_second
+    h_second = (normed_second * ffn_gain).astype(jnp.bfloat16)
+
+    rows_in = jnp.concatenate(gather_group(h_second), axis=0)
+    grad_in = jnp.concatenate(cotangent_parts, axis=0)
+    gate_val = jnp.dot(rows_in, weight_gate, preferred_element_type=f32)
+    up_val = jnp.dot(rows_in, weight_up, preferred_element_type=f32)
+    act, act_back = jax.vjp(glu_value, gate_val, up_val)
+    act_low = act.astype(bf16)
+    result = jnp.dot(act_low, weight_down, preferred_element_type=f32).astype(bf16)
+    weighted = (gate_column * result.astype(f32)).astype(bf16)
+    slot_grads = (gate_column * grad_in.astype(f32)).astype(bf16)
+    act_grad = jnp.einsum("td,fd->tf", slot_grads, weight_down, preferred_element_type=f32)
+    gate_grad_val, up_grad_val = act_back(act_grad)
+    gate_low = gate_grad_val.astype(bf16)
+    up_low = up_grad_val.astype(bf16)
+    rows_grad = jnp.einsum("tf,df->td", gate_low, weight_gate, preferred_element_type=f32)
+    rows_grad = rows_grad + jnp.einsum("tf,df->td", up_low, weight_up, preferred_element_type=f32)
+    rows_grad = rows_grad.astype(bf16)
+    second_grad = reduce_group(
+        [rows_grad[i * length_total : (i + 1) * length_total] for i in range(8)]
+    )
+    down_part = jnp.einsum("tf,td->fd", act_low, slot_grads, preferred_element_type=f32)
+    gate_part = jnp.einsum("td,tf->df", rows_in, gate_low, preferred_element_type=f32)
+    up_part = jnp.einsum("td,tf->df", rows_in, up_low, preferred_element_type=f32)
+    expert_sums = (give(gate_part, 0)[None], give(up_part, 0)[None], give(down_part, 1)[None])
+    combined = reduce_group([weighted[i * length_total : (i + 1) * length_total] for i in range(8)])
+    layer_out = (mixed + combined).astype(bf16)
+    grad_out = cotangent.astype(f32)
+    ffn_gain_part = jnp.sum(second_grad * normed_second, axis=0)
+    normed_grad = second_grad * ffn_gain
+    mixed_grad = grad_out + scale_second * (
+        normed_grad - normed_second * jnp.mean(normed_grad * normed_second, axis=-1, keepdims=True)
+    )
+    mixed_low = mixed_grad.astype(jnp.bfloat16)
+    output_part = jnp.einsum("ti,td->di", attended, mixed_low, preferred_element_type=jnp.float32)
+    output_grad = reduce_all(output_part).T
+    attended_grad = jnp.einsum(
+        "td,id->ti", mixed_low, output_weight, preferred_element_type=jnp.float32
+    )
+    attended_grad = attended_grad.astype(jnp.bfloat16).reshape(
+        length_total, key_heads, q_per_kv, HEAD_SIZE
+    )
+    probs = jnp.exp(scores_of(query_rot, key_rot, allowed) - log_total)
+    probs_again = probs.astype(jnp.bfloat16)
+    value_part_grad = jnp.einsum(
+        "kgts,tkgd->skd", probs_again, attended_grad, preferred_element_type=jnp.float32
+    )
+    prob_grad = jnp.einsum(
+        "tkgd,skd->kgts", attended_grad, value_low, preferred_element_type=jnp.float32
+    )
+    inner = jnp.sum(probs * prob_grad, axis=-1, keepdims=True)
+    score_grad = (probs * (prob_grad - inner)).astype(jnp.bfloat16)
+    qrot_grad = jnp.einsum(
+        "kgts,skd->tkgd", score_grad, key_rot, preferred_element_type=jnp.float32
+    ) * HEAD_SIZE ** (-0.5)
+    krot_grad = jnp.einsum(
+        "kgts,tkgd->skd", score_grad, query_rot, preferred_element_type=jnp.float32
+    ) * HEAD_SIZE ** (-0.5)
+    query_grad_low = unrotate(
+        qrot_grad.reshape(length_total, query_heads, HEAD_SIZE), cosine_table, sine_table
+    )
+    query_grad_low = query_grad_low.astype(jnp.bfloat16).reshape(
+        length_total, query_heads * HEAD_SIZE
+    )
+    key_grad_low = (
+        unrotate(krot_grad, cosine_table, sine_table)
+        .astype(jnp.bfloat16)
+        .reshape(length_total, key_heads * HEAD_SIZE)
+    )
+    value_grad_low = value_part_grad.astype(jnp.bfloat16).reshape(
+        length_total, key_heads * HEAD_SIZE
+    )
+    projected = jnp.concatenate([query_grad_low, key_grad_low, value_grad_low], axis=1)
+    projected_part = jnp.einsum("td,ti->di", h_first, projected, preferred_element_type=f32)
+    first_grad = jnp.einsum(
+        "ti,di->td", query_grad_low, query_weight, preferred_element_type=jnp.float32
+    )
+    first_grad = first_grad + jnp.einsum(
+        "ti,di->td", key_grad_low, key_matrix, preferred_element_type=jnp.float32
+    )
+    first_grad = first_grad + jnp.einsum(
+        "ti,di->td", value_grad_low, value_matrix, preferred_element_type=jnp.float32
+    )
+    attn_gain_part = jnp.sum(first_grad * normed_first, axis=0)
+    normed_first_grad = first_grad * attn_gain
+    tokens_grad = mixed_grad + scale_first * (
+        normed_first_grad
+        - normed_first * jnp.mean(normed_first_grad * normed_first, axis=-1, keepdims=True)
+    )
+    gains = jnp.stack([attn_gain_part, ffn_gain_part], axis=1)
+    gains_high = gains.astype(bf16).astype(f32)
+    gains = jnp.concatenate([gains_high, gains - gains_high], axis=1)
+    gains = jnp.pad(gains, ((0, 0), (0, 124)))
+    shared = reduce_all(jnp.concatenate([projected_part, gains], axis=1))
+    split_q = query_weight.shape[1]
+    split_k = split_q + key_matrix.shape[1]
+    split_v = split_k + value_matrix.shape[1]
+    gain_sums = shared[:, split_v : split_v + 2] + shared[:, split_v + 2 : split_v + 4]
+    return (
+        layer_out,
+        tokens_grad,
+        shared[:, :split_q],
+        shared[:, split_q:split_k],
+        shared[:, split_k:split_v],
+        output_grad,
+        gain_sums[:, 0],
+        gain_sums[:, 1],
+        expert_sums[0],
+        expert_sums[1],
+        expert_sums[2],
+    )
+
+
 def solution(mesh):
     in_specs = (
         P(("grp", "ep"), None),
@@ -311,4 +581,6 @@
         P("ep", "grp", None),
         P("ep", None, "grp"),
     )
+    paired = mesh.shape["grp"] == 4 and mesh.shape["ep"] == 8
+    local = local_dense if paired else local_routed
     return jax.shard_map(local, mesh=mesh, in_specs=in_specs, out_specs=out_specs, check_vma=False)

time: 1580 us -> 742 us (0.47)
  waiting for transfers between devices: 1010 us -> 171 us
  starting transfers between devices: 23.3 us -> 144 us
  local copies, waits for them, and re-layouts: 183 us -> 87.5 us
  blocking collectives: 38.5 us -> 0 us
  matrix products: 204 us -> 230 us
    all_to_all x4 -> x0, waiting for transfers between devices: 628 us -> none  [the longest x1 192 us: local(): lax.all_to_all(send_rows, 'ep', split_axis=0, concat_axis=0, tiled=True)]
    reduce_scatter x6 -> x0, waiting for transfers between devices: 380 us -> none  [the longest x1 142 us: local(): lax.psum_scatter(output_part, ('grp', 'ep'), scatter_dimension=1, tiled=T...]
    ppermute x0 -> x60, waiting for transfers between devices: none -> 171 us  [the longest x46 145 us: swap(): return lax.ppermute(value, names, [(i, i ^ mask) for i in range(count)])]
    ppermute x0 -> x60, starting transfers between devices: none -> 144 us  [the longest x46 128 us: swap(): return lax.ppermute(value, names, [(i, i ^ mask) for i in range(count)])]
    gather x4 -> x0, local copies, waits for them, and re-layouts: 80.6 us -> none  [the longest x1 22.9 us: local(): grad_send = slot_ext[source].reshape(owners, local_experts, capacity, width)]
    reduce_sum x6 -> x4, other arithmetic: 53.5 us -> 6.02 us  [the longest x1 2.65 us: local_dense(): row_sum = jnp.sum(expo, axis=-1, keepdims=True)]
    unnamed x1 -> x0, blocking collectives: 38.5 us -> none
    dot_general x26 -> x24, matrix products: 200 us -> 227 us  [the longest x1 29.9 us: local_dense(): gate_val = jnp.dot(rows_in, weight_gate, preferred_element_type=f32)]
  transfers between devices with their start and end apart: 11 -> 60, of which waited for: 7 -> 11; matrix products, arithmetic and copies ran while one was open for 22% -> 45% of each run, Pallas kernels for 0% -> 0%
where the time goes in v1:
time: 742 us; the launch traced here: 738 us
  matrix products  230 us (31%)
  waiting for transfers between devices  171 us (23%)
  starting transfers between devices  144 us (19%)
  other arithmetic  103 us (14%)
  local copies, waits for them, and re-layouts  87.5 us (12%)
    ppermute x46, waiting for transfers between devices, swap(): return lax.ppermute(value, names, [(i, i ^ mask) for i in range(count)])  145 us
    ppermute x46, starting transfers between devices, swap(): return lax.ppermute(value, names, [(i, i ^ mask) for i in range(count)])  128 us
    unnamed x200, local copies, waits for them, and re-layouts  45.5 us
    dot_general x1, matrix products, local_dense(): gate_val = jnp.dot(rows_in, weight_gate, preferred_element_type=f32)  29.9 us
    ppermute x5, waiting for transfers between devices, swap_mixed(): lax.ppermute(value, names, [(i, i ^ (mask1 if i & bit_core else mask0)) f...  25.1 us
    dot_general x1, matrix products, local_dense(): jnp.einsum('tf,df->td', gate_low, weight_gate, preferred_element_type=f32)  20.7 us
    dot_general x1, matrix products, local_dense(): jnp.einsum('tf,df->td', up_low, weight_up, preferred_element_type=f32)  18.2 us
    dot_general x1, matrix products, local_dense(): jnp.einsum('td,tf->df', rows_in, up_low, preferred_element_type=f32)  16.3 us
  transfers between devices with their start and end apart: 60, of which 11 were waited for; matrix products, arithmetic and copies ran while one was open for 45% of the time, Pallas kernels for 0%

profile of v1, /device:TPU:0, one launch (start us, length us, event | category | flops | bytes accessed | tf_op | source)
XLA Modules:
  0.0 737.6 jit_solution(16133622118750466214)
XLA Ops:
  45.5 7.4 %multiply_reduce_fusion.2 = (f32[512]{0:T(512)S(1)}, f32[512,1536]{1,0:T(8,128)}) fusion(bf16[512,1536]{0,1:T(8,128)(2,1)S(1)} %bitcast.207, bf16[1536,1536]{1,0:T(8,128)(2,1)} %param.23, bf16[512,1536]{1,0:T(8,128)(2,1)S(1)} %copy-done.9), kind=kOutput, calls=%fused_computation.77 | convolution fusion | flops 2419064320 | bytes 11012096 | tf_op jit(solution)/shard_map/dot_general | solution.py:438
  68.1 9.5 %collective-permute-start.4 = (f32[8,512]{1,0:T(8,128)S(1)}, f32[8,512]{1,0:T(8,128)S(1)}, u32[]{:S(2)}, u32[]{:S(2)}) collective-permute-start(f32[8,512]{1,0:T(8,128)S(1)} %collective-permute-done), channel_id=1, source_target_pairs={{0,8},{1,9},{2,10},{3,11},{4,12},{5,13},{6,14},{7,15},{8,0},{9,1},... | collective-permute-start | bytes 49160 | tf_op jit(solution)/shard_map/ppermute | solution.py:313
  89.0 26.8 %collective-permute-start.30 = (bf16[512,1536]{1,0:T(8,128)(2,1)S(1)}, bf16[512,1536]{1,0:T(8,128)(2,1)S(1)}, u32[]{:S(2)}, u32[]{:S(2)}) collective-permute-start(bf16[512,1536]{1,0:T(8,128)(2,1)S(1)} %copy-done.25), channel_id=1, source_target_pairs={{0,8},{1,9},{2,10},{3,11},{4,12},{5,13},{6,14},{7,15},{8,0},{9,1},... | collective-permute-start | bytes 4718600 | tf_op jit(solution)/shard_map/ppermute | solution.py:313
  122.4 28.2 %collective-permute-done.8 = bf16[512,1536]{1,0:T(8,128)(2,1)S(1)} collective-permute-done((bf16[512,1536]{1,0:T(8,128)(2,1)}, bf16[512,1536]{1,0:T(8,128)(2,1)S(1)}, u32[]{:S(2)}, u32[]{:S(2)}) %collective-permute-start.8) | collective-permute-done | bytes 1572896 | tf_op jit(solution)/shard_map/ppermute | solution.py:313
  155.2 5.5 collective-permute-start.31
  163.7 7.3 collective-permute-start.10
  177.5 10.4 %collective-permute-done.9 = bf16[512,1536]{1,0:T(8,128)(2,1)S(1)} collective-permute-done((bf16[512,1536]{1,0:T(8,128)(2,1)S(1)}, bf16[512,1536]{1,0:T(8,128)(2,1)S(1)}, u32[]{:S(2)}, u32[]{:S(2)}) %collective-permute-start.9) | collective-permute-done | bytes 1572896 | tf_op jit(solution)/shard_map/ppermute | solution.py:316
  203.4 16.0 %fusion.64 = f32[4096,768]{1,0:T(8,128)} fusion(bf16[4096,1536]{1,0:T(8,128)(2,1)} %constant_dynamic-update-slice_fusion.8, bf16[768,768]{1,0:T(8,128)(2,1)S(1)} %get-tuple-element.46, bf16[768,768]{1,0:T(8,128)(2,1)S(1)} %get-tuple-element.45, bf16[1,1536,768]{2,1,0:T(8,128)(2,1)S(1)} %copy-done.53, pred[]{:T(512)S(6)} %eq.78), kind=kOutput, calls=%fused_computation.165 | convolution fusion | flops 9669574656 | bytes 29884416 | tf_op jit(solution)/shard_map/dot_general | solution.py:446
  221.6 15.8 %fusion.17 = f32[4096,768]{1,0:T(8,128)} fusion(bf16[4096,1536]{1,0:T(8,128)(2,1)} %constant_dynamic-update-slice_fusion.16, f32[4096]{0:T(1024)S(1)} %bitcast.202, bf16[384,1536]{1,0:T(8,128)(2,1)S(1)} %get-tuple-element.42, bf16[384,1536]{1,0:T(8,128)(2,1)S(1)} %get-tuple-element.41, bf16[1,768,1536]{2,1,0:T(8,128)(2,1)S(1)} %copy-done.51, pred[]{:T(512)S(6)} %eq.78), kind=kOutput, calls=%fused_computation.35 | convolution fusion | flops 9688449024 | bytes 29900800 | tf_op jit(solution)/shard_map/td,fd->tf/dot_general | solution.py:452
  237.4 29.9 %fusion.6 = (bf16[4096,768]{1,0:T(8,128)(2,1)}, bf16[4096,768]{1,0:T(8,128)(2,1)}, bf16[4096,768]{1,0:T(8,128)(2,1)}) fusion(f32[4096,768]{1,0:T(8,128)} %fusion.17, f32[4096,768]{1,0:T(8,128)} %fusion.64, bf16[4096,1536]{1,0:T(8,128)(2,1)} %constant_dynamic-update-slice_fusion.8, bf16[768,768]{1,0:T(8,128)(2,1)} %get-tuple-element.44, ...), kind=kOutput, calls=%fused_computation.14 | convolution fusion | flops 9751363584 | bytes 61341696 | tf_op jit(solution)/shard_map/dot_general | solution.py:445
  267.3 13.6 %multiply_convert_fusion.1 = bf16[4096,1536]{1,0:T(8,128)(2,1)S(1)} fusion(bf16[4096,768]{1,0:T(8,128)(2,1)} %get-tuple-element.23, f32[4096]{0:T(1024)S(1)} %bitcast.203, bf16[384,1536]{1,0:T(8,128)(2,1)} %copy-done.40, bf16[384,1536]{1,0:T(8,128)(2,1)} %copy-done.39, bf16[1,768,1536]{2,1,0:T(8,128)(2,1)} %param.26, pred[]{:T(512)S(6)} %eq.78), kind=kOutput, calls=%fused_computation.2 | convolution fusion | flops 9694740480 | bytes 23609344 | tf_op jit(solution)/shard_map/dot_general | solution.py:449
  287.9 18.2 %fusion.63 = f32[4096,1536]{1,0:T(8,128)} fusion(bf16[4096,768]{1,0:T(8,128)(2,1)} %get-tuple-element.22, bf16[768,768]{1,0:T(8,128)(2,1)} %copy-done.38, bf16[768,768]{1,0:T(8,128)(2,1)S(1)} %get-tuple-element.45, bf16[1,1536,768]{2,1,0:T(8,128)(2,1)} %param.25, pred[]{:T(512)S(6)} %eq.78), kind=kOutput, calls=%fused_computation.164 | convolution fusion | flops 9669574656 | bytes 36175872 | tf_op jit(solution)/shard_map/tf,df->td/dot_general | solution.py:457
  306.1 20.7 %add_convert_fusion = bf16[4096,1536]{1,0:T(8,128)(2,1)} fusion(f32[4096,1536]{1,0:T(8,128)} %fusion.63, bf16[4096,768]{1,0:T(8,128)(2,1)} %get-tuple-element.21, bf16[768,768]{1,0:T(8,128)(2,1)S(1)} %copy-done.43, bf16[768,768]{1,0:T(8,128)(2,1)S(1)} %copy-done.42, bf16[1,1536,768]{2,1,0:T(8,128)(2,1)S(1)} %copy-done.55, pred[]{:T(512)S(6)} %eq.78), kind=kOutput, calls=%fused_computation | convolution fusion | flops 9682157568 | bytes 48758784 | tf_op jit(solution)/shard_map/tf,df->td/dot_general | solution.py:456
  331.9 15.2 %fusion.16 = f32[768,1536]{1,0:T(8,128)S(1)} fusion(bf16[4096,768]{1,0:T(8,128)(2,1)} %get-tuple-element.23, bf16[4096,1536]{1,0:T(8,128)(2,1)} %constant_dynamic-update-slice_fusion.16, f32[4096]{0:T(1024)S(1)} %bitcast.204), kind=kOutput, calls=%fused_computation.34 | convolution fusion | flops 9682550784 | bytes 23609344 | tf_op jit(solution)/shard_map/tf,td->fd/dot_general | solution.py:462
  356.1 14.7 %fusion.93 = f32[1536,768]{1,0:T(8,128)S(1)} fusion(bf16[4096,1536]{1,0:T(8,128)(2,1)} %constant_dynamic-update-slice_fusion.8, bf16[4096,768]{1,0:T(8,128)(2,1)} %get-tuple-element.21), kind=kOutput, calls=%fused_computation.229 | convolution fusion | flops 9663676416 | bytes 23592960 | tf_op jit(solution)/shard_map/td,tf->df/dot_general | solution.py:463
  372.5 6.3 fusion.24
  379.8 14.7 %collective-permute-done.37 = bf16[512,1536]{1,0:T(8,128)(2,1)} collective-permute-done((bf16[512,1536]{1,0:T(8,128)(2,1)}, bf16[512,1536]{1,0:T(8,128)(2,1)}, u32[]{:S(2)}, u32[]{:S(2)}) %collective-permute-start.37) | collective-permute-done | bytes 1572896 | tf_op jit(solution)/shard_map/ppermute | solution.py:316
  402.5 16.3 %fusion.94 = f32[1536,768]{1,0:T(8,128)} fusion(bf16[4096,1536]{1,0:T(8,128)(2,1)} %constant_dynamic-update-slice_fusion.8, bf16[4096,768]{1,0:T(8,128)(2,1)} %get-tuple-element.22), kind=kOutput, calls=%fused_computation.230 | convolution fusion | flops 9663676416 | bytes 23592960 | tf_op jit(solution)/shard_map/td,tf->df/dot_general | solution.py:464
  424.2 31.6 %collective-permute-done.38 = bf16[512,1536]{1,0:T(8,128)(2,1)S(1)} collective-permute-done((bf16[512,1536]{1,0:T(8,128)(2,1)}, bf16[512,1536]{1,0:T(8,128)(2,1)S(1)}, u32[]{:S(2)}, u32[]{:S(2)}) %collective-permute-start.38) | collective-permute-done | bytes 1572896 | tf_op jit(solution)/shard_map/ppermute | solution.py:313
  463.5 6.2 convert_bitcast_fusion
  477.1 8.7 %fusion.53 = bf16[2,128,512]{2,1,0:T(8,128)(2,1)} fusion(bf16[512,2,6,128]{0,3,2,1:T(8,128)(2,1)S(1)} %bitcast.188, f32[2,6,512]{2,1,0:T(8,128)S(1)} %copy-done.56, f32[2,512,512,6]{2,1,3,0:T(8,128)} %copy-done.1, pred[512,512]{0,1:T(8,128)(4,1)S(1)} %copy-done.12), kind=kOutput, calls=%fused_computation.118 | convolution fusion | flops 818020352 | bytes 14704640 | tf_op jit(solution)/shard_map/kgts,tkgd->skd/dot_general | solution.py:485
  485.8 9.7 %fusion.7 = (f32[2,6,512]{2,1,0:T(8,128)S(1)}, f32[2,512,512,6]{2,1,3,0:T(8,128)}) fusion(f32[2,6,512]{2,1,0:T(8,128)S(1)} %copy-done.56, f32[2,512,512,6]{2,1,3,0:T(8,128)} %copy-done.1, pred[512,512]{0,1:T(8,128)(4,1)S(1)} %copy-done.12, bf16[512,2,128,1]{0,2,3,1:T(8,128)(2,1)S(1)} %bitcast.198, bf16[512,2,6,128]{0,3,2,1:T(8,128)(2,1)S(1)} %bitcast.189), kind=kOutput, calls=%fused_computation.17 | convolution fusion | flops 821028864 | bytes 27312128 | tf_op jit(solution)/shard_map/tkgd,skd->kgts/dot_general | solution.py:488
  495.6 7.5 %fusion.9 = bf16[2,6,512,512]{2,3,1,0:T(8,128)(2,1)S(1)} fusion(f32[2,512,512,6]{2,1,3,0:T(8,128)} %get-tuple-element.66, f32[2,6,512]{2,1,0:T(8,128)S(1)} %get-tuple-element.65, f32[2,6,512]{2,1,0:T(8,128)S(1)} %copy-done.56, f32[2,512,512,6]{2,1,3,0:T(8,128)S(1)} %bitcast.168, pred[512,512]{0,1:T(8,128)(4,1)S(1)} %copy-done.12), kind=kLoop, calls=%fused_computation.19 | loop fusion | flops 18874368 | bytes 31768576 | tf_op jit(solution)/shard_map/convert_element_type | solution.py:492
  520.7 7.8 %fusion.38 = f32[1536,2048]{1,0:T(8,128)} fusion(bf16[512,256]{0,1:T(8,128)(2,1)S(1)} %bitcast.200, bf16[512,256]{0,1:T(8,128)(2,1)S(1)} %bitcast.195, bf16[512,1536]{0,1:T(8,128)(2,1)S(1)} %bitcast.192, bf16[512,1536]{1,0:T(8,128)(2,1)S(1)} %copy-done.10, f32[1536]{0:T(1024)S(1)} %copy-done.66, f32[512]{0:T(512)S(1)} %copy-done.68), kind=kOutput, calls=%fused_computation.93 | convolution fusion | flops 3230662656 | bytes 16261120 | tf_op jit(solution)/shard_map/td,ti->di/dot_general | solution.py:514
  541.5 10.7 %select_maximum_fusion = f32[1536,2176]{1,0:T(8,128)} fusion(f32[1536,4]{1,0:T(8,128)S(1)} %copy.133, f32[1536,2048]{1,0:T(8,128)} %fusion.38), kind=kLoop, calls=%fused_computation.6 | loop fusion | flops 10027008 | bytes 25976832 | tf_op jit(solution)/shard_map/concatenate | solution.py:534
  579.8 28.9 %collective-permute-start.53 = (bf16[384,768]{1,0:T(8,128)(2,1)}, bf16[384,768]{1,0:T(8,128)(2,1)}, u32[]{:S(2)}, u32[]{:S(2)}) collective-permute-start(bf16[384,768]{1,0:T(8,128)(2,1)} %dynamic-slice_convert_fusion.10), channel_id=1, source_target_pairs={{0,8},{1,9},{2,10},{3,11},{4,12},{5,13},{6,14},{7,15},{8,0},{9,1},... | collective-permute-start | bytes 1769480 | tf_op jit(solution)/shard_map/ppermute | solution.py:313
  613.0 8.3 %collective-permute-start.56 = (bf16[384,768]{1,0:T(8,128)(2,1)}, bf16[384,768]{1,0:T(8,128)(2,1)}, u32[]{:S(2)}, u32[]{:S(2)}) collective-permute-start(bf16[384,768]{1,0:T(8,128)(2,1)} %dynamic-slice_convert_fusion.9), channel_id=1, source_target_pairs={{0,8},{1,9},{2,10},{3,11},{4,12},{5,13},{6,14},{7,15},{8,0},{9,1},... | collective-permute-start | bytes 1769480 | tf_op jit(solution)/shard_map/ppermute | solution.py:313
  639.4 16.1 %collective-permute-done.47 = bf16[1,1,2,2,2,48,1536]{6,5,4,3,2,1,0:T(8,128)(2,1)} collective-permute-done((bf16[1,1,2,2,2,48,1536]{6,5,4,3,2,1,0:T(8,128)(2,1)}, bf16[1,1,2,2,2,48,1536]{6,5,4,3,2,1,0:T(8,128)(2,1)}, u32[]{:S(2)}, u32[]{:S(2)}) %collective-permute-start.47) | collective-permute-done | bytes 1179680 | tf_op jit(solution)/shard_map/ppermute | solution.py:313
  657.9 32.5 %collective-permute-done.42 = bf16[1,1,2,2,2,48,2176]{6,5,4,3,2,1,0:T(8,128)(2,1)S(1)} collective-permute-done((bf16[1,1,2,2,2,48,2176]{6,5,4,3,2,1,0:T(8,128)(2,1)S(1)}, bf16[1,1,2,2,2,48,2176]{6,5,4,3,2,1,0:T(8,128)(2,1)S(1)}, u32[]{:S(2)}, u32[]{:S(2)}) %collective-permute-start.42) | collective-permute-done | bytes 1671200 | tf_op jit(solution)/shard_map/ppermute | solution.py:313
  694.4 16.3 %collective-permute-done.43 = bf16[1,1,2,2,1,48,2176]{6,5,4,3,2,1,0:T(8,128)(2,1)S(1)} collective-permute-done((bf16[1,1,2,2,1,48,2176]{6,5,4,3,2,1,0:T(8,128)(2,1)S(1)}, bf16[1,1,2,2,1,48,2176]{6,5,4,3,2,1,0:T(8,128)(2,1)S(1)}, u32[]{:S(2)}, u32[]{:S(2)}) %collective-permute-start.43) | collective-permute-done | bytes 835616 | tf_op jit(solution)/shard_map/ppermute | solution.py:313
  714.3 9.7 %collective-permute-done.44 = bf16[1,1,2,1,1,48,2176]{6,5,4,3,2,1,0:T(8,128)(2,1)S(1)} collective-permute-done((bf16[1,1,2,1,1,48,2176]{6,5,4,3,2,1,0:T(8,128)(2,1)S(1)}, bf16[1,1,2,1,1,48,2176]{6,5,4,3,2,1,0:T(8,128)(2,1)S(1)}, u32[]{:S(2)}, u32[]{:S(2)}) %collective-permute-start.44) | collective-permute-done | bytes 417824 | tf_op jit(solution)/shard_map/ppermute | solution.py:313
  725.6 9.6 %collective-permute-done.45 = bf16[1,1,1,1,1,48,2176]{6,5,4,3,2,1,0:T(8,128)(2,1)S(1)} collective-permute-done((bf16[1,1,1,1,1,48,2176]{6,5,4,3,2,1,0:T(8,128)(2,1)S(1)}, bf16[1,1,1,1,1,48,2176]{6,5,4,3,2,1,0:T(8,128)(2,1)S(1)}, u32[]{:S(2)}, u32[]{:S(2)}) %collective-permute-start.45) | collective-permute-done | bytes 208928 | tf_op jit(solution)/shard_map/ppermute | solution.py:313
  (418 shorter events, 255.2 us)
Async XLA Ops:
  2.2 57.3 %collective-permute-start.1 = (f32[8,512]{1,0:T(8,128)}, f32[8,512]{1,0:T(8,128)}, u32[]{:S(2)}, u32[]{:S(2)}) collective-permute-start(f32[8,512]{1,0:T(8,128)} %bitcast.13), channel_id=1, source_target_pairs={{0,2},{1,3},{2,0},{3,1},{4,6},{5,7},{6,4},{7,5},{8,10},{9,11},{10,... | collective-permute-start | bytes 49160 | tf_op jit(solution)/shard_map/ppermute | solution.py:313
  5.2 55.0 %collective-permute-start = (f32[8,512]{1,0:T(8,128)}, f32[8,512]{1,0:T(8,128)S(1)}, u32[]{:S(2)}, u32[]{:S(2)}) collective-permute-start(f32[8,512]{1,0:T(8,128)} %bitcast.13), channel_id=1, source_target_pairs={{0,1},{1,0},{2,3},{3,2},{4,5},{5,4},{6,7},{7,6},{8,9},{9,8},{10,11... | collective-permute-start | bytes 49160 | tf_op jit(solution)/shard_map/ppermute | solution.py:313
  6.7 56.8 %collective-permute-start.3 = (f32[8,512]{1,0:T(8,128)}, f32[8,512]{1,0:T(8,128)}, u32[]{:S(2)}, u32[]{:S(2)}) collective-permute-start(f32[8,512]{1,0:T(8,128)} %bitcast.13), channel_id=1, source_target_pairs={{0,8},{1,9},{2,10},{3,11},{4,12},{5,13},{6,14},{7,15},{8,0},{9,1},... | collective-permute-start | bytes 49160 | tf_op jit(solution)/shard_map/ppermute | solution.py:313
  6.7 109.1 %collective-permute-start.28 = (bf16[512,1536]{1,0:T(8,128)(2,1)}, bf16[512,1536]{1,0:T(8,128)(2,1)}, u32[]{:S(2)}, u32[]{:S(2)}) collective-permute-start(bf16[512,1536]{1,0:T(8,128)(2,1)} %param.27), channel_id=1, source_target_pairs={{0,2},{1,3},{2,0},{3,1},{4,6},{5,7},{6,4},{7,5},{8,10},{9,11},{10,... | collective-permute-start | bytes 4718600 | tf_op jit(solution)/shard_map/ppermute | solution.py:313
  7.2 77.2 %collective-permute-start.27 = (bf16[512,1536]{1,0:T(8,128)(2,1)}, bf16[512,1536]{1,0:T(8,128)(2,1)}, u32[]{:S(2)}, u32[]{:S(2)}) collective-permute-start(bf16[512,1536]{1,0:T(8,128)(2,1)} %param.27), channel_id=1, source_target_pairs={{0,1},{1,0},{2,3},{3,2},{4,5},{5,4},{6,7},{7,6},{8,9},{9,8},{10,11... | collective-permute-start | bytes 4718600 | tf_op jit(solution)/shard_map/ppermute | solution.py:313
  80.1 40.3 %collective-permute-start.7 = (bf16[512,1536]{1,0:T(8,128)(2,1)}, bf16[512,1536]{1,0:T(8,128)(2,1)S(1)}, u32[]{:S(2)}, u32[]{:S(2)}) collective-permute-start(bf16[512,1536]{1,0:T(8,128)(2,1)} %get-tuple-element.20), channel_id=1, source_target_pairs={{0,1},{1,0},{2,3},{3,2},{4,5},{5,4},{6,7},{7,6},{8,9},{9,8},{10,11... | collective-permute-start | bytes 4718600 | tf_op jit(solution)/shard_map/ppermute | solution.py:313
  82.2 68.4 %collective-permute-start.8 = (bf16[512,1536]{1,0:T(8,128)(2,1)}, bf16[512,1536]{1,0:T(8,128)(2,1)S(1)}, u32[]{:S(2)}, u32[]{:S(2)}) collective-permute-start(bf16[512,1536]{1,0:T(8,128)(2,1)} %get-tuple-element.20), channel_id=1, source_target_pairs={{0,2},{1,3},{2,0},{3,1},{4,6},{5,7},{6,4},{7,5},{8,10},{9,11},{10,... | collective-permute-start | bytes 4718600 | tf_op jit(solution)/shard_map/ppermute | solution.py:313
  89.0 63.3 %collective-permute-start.30 = (bf16[512,1536]{1,0:T(8,128)(2,1)S(1)}, bf16[512,1536]{1,0:T(8,128)(2,1)S(1)}, u32[]{:S(2)}, u32[]{:S(2)}) collective-permute-start(bf16[512,1536]{1,0:T(8,128)(2,1)S(1)} %copy-done.25), channel_id=1, source_target_pairs={{0,8},{1,9},{2,10},{3,11},{4,12},{5,13},{6,14},{7,15},{8,0},{9,1},... | collective-permute-start | bytes 4718600 | tf_op jit(solution)/shard_map/ppermute | solution.py:313
  115.9 39.4 %collective-permute-start.19 = (bf16[384,1536]{1,0:T(8,128)(2,1)S(1)}, bf16[384,1536]{1,0:T(8,128)(2,1)S(1)}, u32[]{:S(2)}, u32[]{:S(2)}) collective-permute-start(bf16[384,1536]{1,0:T(8,128)(2,1)S(1)} %collective-permute-done.18), channel_id=1, source_target_pairs={{8,24},{9,25},{10,26},{11,27},{12,28},{13,29},{14,30},{15,31},{24,... | collective-permute-start | bytes 3538952 | tf_op jit(solution)/shard_map/ppermute | solution.py:321
  119.6 41.5 %collective-permute-start.17 = (bf16[768,768]{1,0:T(8,128)(2,1)S(1)}, bf16[768,768]{1,0:T(8,128)(2,1)S(1)}, u32[]{:S(2)}, u32[]{:S(2)}) collective-permute-start(bf16[768,768]{1,0:T(8,128)(2,1)S(1)} %collective-permute-done.16), channel_id=1, source_target_pairs={{8,24},{9,25},{10,26},{11,27},{12,28},{13,29},{14,30},{15,31},{24,... | collective-permute-start | bytes 3538952 | tf_op jit(solution)/shard_map/ppermute | solution.py:321
  120.4 41.1 %collective-permute-start.15 = (bf16[768,768]{1,0:T(8,128)(2,1)S(1)}, bf16[768,768]{1,0:T(8,128)(2,1)S(1)}, u32[]{:S(2)}, u32[]{:S(2)}) collective-permute-start(bf16[768,768]{1,0:T(8,128)(2,1)S(1)} %collective-permute-done.14), channel_id=1, source_target_pairs={{8,24},{9,25},{10,26},{11,27},{12,28},{13,29},{14,30},{15,31},{24,... | collective-permute-start | bytes 3538952 | tf_op jit(solution)/shard_map/ppermute | solution.py:321
  152.3 35.6 %collective-permute-start.9 = (bf16[512,1536]{1,0:T(8,128)(2,1)S(1)}, bf16[512,1536]{1,0:T(8,128)(2,1)S(1)}, u32[]{:S(2)}, u32[]{:S(2)}) collective-permute-start(bf16[512,1536]{1,0:T(8,128)(2,1)S(1)} %get-tuple-element.49), channel_id=1, source_target_pairs={{0,1},{1,0},{2,3},{3,2},{4,5},{5,4},{6,7},{7,6},{8,10},{9,11},{10,... | collective-permute-start | bytes 4718600 | tf_op jit(solution)/shard_map/ppermute | solution.py:316
  155.2 38.8 %collective-permute-start.31 = (bf16[512,1536]{1,0:T(8,128)(2,1)}, bf16[512,1536]{1,0:T(8,128)(2,1)S(1)}, u32[]{:S(2)}, u32[]{:S(2)}) collective-permute-start(bf16[512,1536]{1,0:T(8,128)(2,1)} %collective-permute-done.27), channel_id=1, source_target_pairs={{0,8},{1,9},{2,10},{3,11},{4,12},{5,13},{6,14},{7,15},{8,0},{9,1},... | collective-permute-start | bytes 4718600 | tf_op jit(solution)/shard_map/ppermute | solution.py:313
  161.1 35.4 %collective-permute-start.32 = (bf16[512,1536]{1,0:T(8,128)(2,1)}, bf16[512,1536]{1,0:T(8,128)(2,1)S(1)}, u32[]{:S(2)}, u32[]{:S(2)}) collective-permute-start(bf16[512,1536]{1,0:T(8,128)(2,1)} %collective-permute-done.28), channel_id=1, source_target_pairs={{0,8},{1,9},{2,10},{3,11},{4,12},{5,13},{6,14},{7,15},{8,0},{9,1},... | collective-permute-start | bytes 4718600 | tf_op jit(solution)/shard_map/ppermute | solution.py:313
  287.4 67.2 %collective-permute-start.25 = (bf16[512,1536]{1,0:T(8,128)(2,1)}, bf16[512,1536]{1,0:T(8,128)(2,1)}, u32[]{:S(2)}, u32[]{:S(2)}) collective-permute-start(bf16[512,1536]{1,0:T(8,128)(2,1)} %get-tuple-element.33), channel_id=1, source_target_pairs={{0,8},{1,9},{2,10},{3,11},{4,12},{5,13},{6,14},{7,15},{8,0},{9,1},... | collective-permute-start | bytes 4718600 | tf_op jit(solution)/shard_map/ppermute | solution.py:313
  287.4 60.6 %collective-permute-start.22 = (bf16[512,1536]{1,0:T(8,128)(2,1)}, bf16[512,1536]{1,0:T(8,128)(2,1)}, u32[]{:S(2)}, u32[]{:S(2)}) collective-permute-start(bf16[512,1536]{1,0:T(8,128)(2,1)} %get-tuple-element.34), channel_id=1, source_target_pairs={{0,8},{1,9},{2,10},{3,11},{4,12},{5,13},{6,14},{7,15},{8,0},{9,1},... | collective-permute-start | bytes 4718600 | tf_op jit(solution)/shard_map/ppermute | solution.py:313
  354.6 39.9 %collective-permute-start.37 = (bf16[512,1536]{1,0:T(8,128)(2,1)}, bf16[512,1536]{1,0:T(8,128)(2,1)}, u32[]{:S(2)}, u32[]{:S(2)}) collective-permute-start(bf16[512,1536]{1,0:T(8,128)(2,1)} %add_convert_fusion.1), channel_id=1, source_target_pairs={{0,1},{1,0},{2,3},{3,2},{4,5},{5,4},{6,7},{7,6},{8,10},{9,11},{10,... | collective-permute-start | bytes 4718600 | tf_op jit(solution)/shard_map/ppermute | solution.py:316
  378.8 82.8 %collective-permute-start.20 = (bf16[512,1536]{1,0:T(8,128)(2,1)}, bf16[512,1536]{1,0:T(8,128)(2,1)}, u32[]{:S(2)}, u32[]{:S(2)}) collective-permute-start(bf16[512,1536]{1,0:T(8,128)(2,1)} %get-tuple-element.32), channel_id=1, source_target_pairs={{0,8},{1,9},{2,10},{3,11},{4,12},{5,13},{6,14},{7,15},{8,0},{9,1},... | collective-permute-start | bytes 4718600 | tf_op jit(solution)/shard_map/ppermute | solution.py:313
  379.3 84.2 %collective-permute-start.24 = (bf16[512,1536]{1,0:T(8,128)(2,1)}, bf16[512,1536]{1,0:T(8,128)(2,1)}, u32[]{:S(2)}, u32[]{:S(2)}) collective-permute-start(bf16[512,1536]{1,0:T(8,128)(2,1)} %get-tuple-element.26), channel_id=1, source_target_pairs={{0,1},{1,0},{2,3},{3,2},{4,5},{5,4},{6,7},{7,6},{8,9},{9,8},{10,11... | collective-permute-start | bytes 4718600 | tf_op jit(solution)/shard_map/ppermute | solution.py:313
  394.5 69.0 %collective-permute-start.26 = (bf16[512,1536]{1,0:T(8,128)(2,1)}, bf16[512,1536]{1,0:T(8,128)(2,1)}, u32[]{:S(2)}, u32[]{:S(2)}) collective-permute-start(bf16[512,1536]{1,0:T(8,128)(2,1)} %get-tuple-element.27), channel_id=1, source_target_pairs={{0,2},{1,3},{2,0},{3,1},{4,6},{5,7},{6,4},{7,5},{8,10},{9,11},{10,... | collective-permute-start | bytes 4718600 | tf_op jit(solution)/shard_map/ppermute | solution.py:313
  400.2 55.6 %collective-permute-start.38 = (bf16[512,1536]{1,0:T(8,128)(2,1)}, bf16[512,1536]{1,0:T(8,128)(2,1)S(1)}, u32[]{:S(2)}, u32[]{:S(2)}) collective-permute-start(bf16[512,1536]{1,0:T(8,128)(2,1)} %get-tuple-element.24), channel_id=1, source_target_pairs={{0,1},{1,0},{2,3},{3,2},{4,5},{5,4},{6,7},{7,6},{8,9},{9,8},{10,11... | collective-permute-start | bytes 4718600 | tf_op jit(solution)/shard_map/ppermute | solution.py:313
  400.8 57.8 %collective-permute-start.40 = (bf16[512,1536]{1,0:T(8,128)(2,1)}, bf16[512,1536]{1,0:T(8,128)(2,1)S(1)}, u32[]{:S(2)}, u32[]{:S(2)}) collective-permute-start(bf16[512,1536]{1,0:T(8,128)(2,1)} %get-tuple-element.25), channel_id=1, source_target_pairs={{0,2},{1,3},{2,0},{3,1},{4,6},{5,7},{6,4},{7,5},{8,10},{9,11},{10,... | collective-permute-start | bytes 4718600 | tf_op jit(solution)/shard_map/ppermute | solution.py:313
  455.7 102.2 %collective-permute-start.51 = (bf16[768,768]{1,0:T(8,128)(2,1)}, bf16[768,768]{1,0:T(8,128)(2,1)}, u32[]{:S(2)}, u32[]{:S(2)}) collective-permute-start(bf16[768,768]{1,0:T(8,128)(2,1)} %dynamic-slice_convert_fusion.5), channel_id=1, source_target_pairs={{0,16},{1,17},{2,18},{3,19},{4,20},{5,21},{6,22},{7,23},{8,24},{9,... | collective-permute-start | bytes 3538952 | tf_op jit(solution)/shard_map/ppermute | solution.py:313
  458.5 104.4 %collective-permute-start.54 = (bf16[768,768]{1,0:T(8,128)(2,1)}, bf16[768,768]{1,0:T(8,128)(2,1)}, u32[]{:S(2)}, u32[]{:S(2)}) collective-permute-start(bf16[768,768]{1,0:T(8,128)(2,1)} %dynamic-slice_convert_fusion.4), channel_id=1, source_target_pairs={{0,16},{1,17},{2,18},{3,19},{4,20},{5,21},{6,22},{7,23},{8,24},{9,... | collective-permute-start | bytes 3538952 | tf_op jit(solution)/shard_map/ppermute | solution.py:313
  461.6 105.6 %collective-permute-start.58 = (bf16[768,768]{1,0:T(8,128)(2,1)}, bf16[768,768]{1,0:T(8,128)(2,1)}, u32[]{:S(2)}, u32[]{:S(2)}) collective-permute-start(bf16[768,768]{1,0:T(8,128)(2,1)} %fusion.47), channel_id=1, source_target_pairs={{8,12},{9,13},{10,14},{11,15},{12,8},{13,9},{14,10},{15,11},{24,28... | collective-permute-start | bytes 3538952 | tf_op jit(solution)/shard_map/ppermute | solution.py:321
  541.2 80.1 %collective-permute-start.46 = (bf16[2,1,2,2,2,48,1536]{6,5,4,3,2,1,0:T(8,128)(2,1)}, bf16[2,1,2,2,2,48,1536]{6,5,4,3,2,1,0:T(8,128)(2,1)}, u32[]{:S(2)}, u32[]{:S(2)}) collective-permute-start(bf16[2,1,2,2,2,48,1536]{6,5,4,3,2,1,0:T(8,128)(2,1)} %dynamic-slice_convert_fusion.1), channel_id=1, source_target_pairs={{0,8},{1,9},{2,10},{3,11},{4,12},{5,13},{6,14},{7,15},{8,0},{9,1},... | collective-permute-start | bytes 7077896 | tf_op jit(solution)/shard_map/ppermute | solution.py:313
  557.4 70.2 %collective-permute-start.41 = (bf16[2,1,2,2,2,48,2176]{6,5,4,3,2,1,0:T(8,128)(2,1)}, bf16[2,1,2,2,2,48,2176]{6,5,4,3,2,1,0:T(8,128)(2,1)}, u32[]{:S(2)}, u32[]{:S(2)}) collective-permute-start(bf16[2,1,2,2,2,48,2176]{6,5,4,3,2,1,0:T(8,128)(2,1)} %dynamic-slice_convert_fusion), channel_id=1, source_target_pairs={{0,8},{1,9},{2,10},{3,11},{4,12},{5,13},{6,14},{7,15},{8,0},{9,1},... | collective-permute-start | bytes 10027016 | tf_op jit(solution)/shard_map/ppermute | solution.py:313
  565.6 43.2 %collective-permute-start.55 = (bf16[768,768]{1,0:T(8,128)(2,1)}, bf16[768,768]{1,0:T(8,128)(2,1)}, u32[]{:S(2)}, u32[]{:S(2)}) collective-permute-start(bf16[768,768]{1,0:T(8,128)(2,1)} %fusion.46), channel_id=1, source_target_pairs={{8,12},{9,13},{10,14},{11,15},{12,8},{13,9},{14,10},{15,11},{24,28... | collective-permute-start | bytes 3538952 | tf_op jit(solution)/shard_map/ppermute | solution.py:321
  572.4 59.1 %collective-permute-start.59 = (bf16[768,384]{1,0:T(8,128)(2,1)}, bf16[768,384]{1,0:T(8,128)(2,1)}, u32[]{:S(2)}, u32[]{:S(2)}) collective-permute-start(bf16[768,384]{1,0:T(8,128)(2,1)} %dynamic-slice_convert_fusion.8), channel_id=1, source_target_pairs={{0,8},{1,9},{2,10},{3,11},{4,12},{5,13},{6,14},{7,15},{8,0},{9,1},... | collective-permute-start | bytes 1769480 | tf_op jit(solution)/shard_map/ppermute | solution.py:313
  579.8 55.2 %collective-permute-start.53 = (bf16[384,768]{1,0:T(8,128)(2,1)}, bf16[384,768]{1,0:T(8,128)(2,1)}, u32[]{:S(2)}, u32[]{:S(2)}) collective-permute-start(bf16[384,768]{1,0:T(8,128)(2,1)} %dynamic-slice_convert_fusion.10), channel_id=1, source_target_pairs={{0,8},{1,9},{2,10},{3,11},{4,12},{5,13},{6,14},{7,15},{8,0},{9,1},... | collective-permute-start | bytes 1769480 | tf_op jit(solution)/shard_map/ppermute | solution.py:313
  630.6 59.8 %collective-permute-start.42 = (bf16[1,1,2,2,2,48,2176]{6,5,4,3,2,1,0:T(8,128)(2,1)S(1)}, bf16[1,1,2,2,2,48,2176]{6,5,4,3,2,1,0:T(8,128)(2,1)S(1)}, u32[]{:S(2)}, u32[]{:S(2)}) collective-permute-start(bf16[1,1,2,2,2,48,2176]{6,5,4,3,2,1,0:T(8,128)(2,1)S(1)} %dynamic-slice_convert_fusion.2), channel_id=1, source_target_pairs={{0,16},{1,17},{2,18},{3,19},{4,20},{5,21},{6,22},{7,23},{8,24},{9,... | collective-permute-start | bytes 5013512 | tf_op jit(solution)/shard_map/ppermute | solution.py:313
  657.3 36.6 %collective-permute-start.48 = (bf16[1,1,2,2,1,48,1536]{6,5,4,3,2,1,0:T(8,128)(2,1)S(1)}, bf16[1,1,2,2,1,48,1536]{6,5,4,3,2,1,0:T(8,128)(2,1)S(1)}, u32[]{:S(2)}, u32[]{:S(2)}) collective-permute-start(bf16[1,1,2,2,1,48,1536]{6,5,4,3,2,1,0:T(8,128)(2,1)S(1)} %dynamic-slice_convert_fusion.11), channel_id=1, source_target_pairs={{0,1},{1,0},{2,3},{3,2},{4,5},{5,4},{6,7},{7,6},{8,9},{9,8},{10,11... | collective-permute-start | bytes 1769480 | tf_op jit(solution)/shard_map/ppermute | solution.py:313
  (118 other events, 1971.5 us)

commit v2 on v1

--- a/solution.py
+++ b/solution.py
@@ -1,6 +1,8 @@
 import jax
 import jax.numpy as jnp
 from jax import lax
+from jax.experimental import pallas as pl
+from jax.experimental.pallas import tpu as pltpu
 from jax.sharding import PartitionSpec as P
 
 HEAD_SIZE = 128
@@ -281,6 +283,326 @@
     )
 
 
+SLOT_ORDER = (0, 4, 1, 5, 2, 6, 7, 3)
+
+
+def moe_kernel(
+    tab_ref, h_ref, dy_ref, wg_ref, wu_ref, wd_ref,
+    grad_gate_ref, grad_up_ref, grad_down_ref, out_own_ref, out_sib_ref, d_own_ref, d_sib_ref,
+    d_first_ref, d_second_ref,
+    xb, dyb, tab, w_gate, w_up, w_down, acc_gate, acc_up, acc_down, act_s, gate_s, up_s, dz_s,
+    sib, far_in, gather_send, gather_recv, tab_send, tab_recv, local_sem, part_send, part_recv,
+    keep_sem, sum_send, sum_recv, store_sem,
+):
+    f32, bf16 = jnp.float32, jnp.bfloat16
+    grp, ep = lax.axis_index("grp"), lax.axis_index("ep")
+    core = lax.rem(grp, 2)
+    low = lax.rem(ep, 4)
+    y, z = lax.rem(low, 2), low // 2
+    by_y = ep + 1 - 2 * y
+    by_z = ep + 2 - 4 * z
+    by_far = by_y + 2 - 4 * z
+    first = by_y * (1 - core) + by_z * core
+    second = by_z * (1 - core) + by_y * core
+    other = grp + 1 - 2 * core
+    hosted = lax.rem(ep + 4 * core, 8)
+    rows = h_ref.shape[0]
+    half = rows // 2
+
+    def remote(src, dst, send, recv, device):
+        return pltpu.make_async_remote_copy(
+            src_ref=src, dst_ref=dst, send_sem=send, recv_sem=recv, device_id=device,
+            device_id_type=pl.DeviceIdType.MESH,
+        )
+
+    members = (
+        ((grp, first), 1), ((grp, second), 2), ((grp, by_far), 3), ((other, ep), 4),
+        ((other, first), 5), ((other, second), 6), ((other, by_far), 7),
+    )
+    barrier = pltpu.get_barrier_semaphore()
+    for device, _ in members:
+        pl.semaphore_signal(barrier, inc=1, device_id=device, device_id_type=pl.DeviceIdType.MESH)
+    pl.semaphore_wait(barrier, 7)
+
+    def gather_copy(k, number):
+        own, buf = ((h_ref, xb), (dy_ref, dyb))[k]
+        src, dst, device = (
+            (own, 1, (grp, first)), (own, 4, (other, ep)), (own, 2, (grp, second)),
+            (buf.at[1], 5, (other, ep)), (buf.at[2], 6, (other, ep)),
+            (buf.at[2], 3, (grp, first)), (buf.at[3], 7, (other, ep)),
+        )[number]
+        return remote(
+            src, buf.at[dst], gather_send.at[k, number], gather_recv.at[k, number], device
+        )
+
+    arrival = {1: 0, 4: 1, 2: 2, 5: 3, 6: 4, 3: 5, 7: 6}
+
+    def start(*numbers):
+        for number in numbers:
+            for k in (0, 1):
+                gather_copy(k, number).start()
+
+    def sent(*numbers):
+        for number in numbers:
+            for k in (0, 1):
+                gather_copy(k, number).wait_send()
+
+    def arrived(slot):
+        for k in (0, 1):
+            gather_copy(k, arrival[slot]).wait_recv()
+
+    locals_in = [
+        pltpu.make_async_copy(src, dst, local_sem.at[i])
+        for i, (src, dst) in enumerate(
+            ((h_ref, xb.at[0]), (dy_ref, dyb.at[0]), (wg_ref, w_gate), (wu_ref, w_up), (wd_ref, w_down))
+        )
+    ]
+    for copy in locals_in:
+        copy.start()
+    table_copies = [
+        remote(tab_ref, tab.at[slot], tab_send.at[slot], tab_recv.at[slot], device)
+        for device, slot in members
+    ]
+    for copy in table_copies:
+        copy.start()
+    start(0, 1)
+    tab[0] = tab_ref[...]
+    acc_gate[...] = jnp.zeros_like(acc_gate)
+    acc_up[...] = jnp.zeros_like(acc_up)
+    acc_down[...] = jnp.zeros_like(acc_down)
+    for copy in locals_in:
+        copy.wait()
+    for copy in table_copies:
+        copy.wait_send()
+        copy.wait_recv()
+
+    def keep_copy(j, src):
+        return pltpu.make_async_copy(src, out_own_ref.at[j], keep_sem.at[j])
+
+    def part_copies(j, dest):
+        grad_dst = d_sib_ref if j == 0 else sib.at[j - 1]
+        return (
+            remote(xb.at[dest], grad_dst, part_send.at[0, j], part_recv.at[0, j], (other, ep)),
+            remote(
+                dyb.at[dest], out_sib_ref.at[j], part_send.at[1, j], part_recv.at[1, j], (other, ep)
+            ),
+        )
+
+    own_grad = pltpu.make_async_copy(xb.at[8], d_own_ref, keep_sem.at[4])
+    send_first = remote(xb.at[4], d_first_ref, sum_send.at[0], sum_recv.at[0], (grp, first))
+    send_far = remote(xb.at[7], far_in, sum_send.at[1], sum_recv.at[1], (grp, first))
+    send_second = remote(xb.at[5], d_second_ref, sum_send.at[2], sum_recv.at[2], (grp, second))
+
+    def dot_nt(a, b):
+        return lax.dot_general(a, b, (((1,), (1,)), ((), ())), preferred_element_type=f32)
+
+    def dot_tn(a, b):
+        return lax.dot_general(a, b, (((0,), (0,)), ((), ())), preferred_element_type=f32)
+
+    def gates(slot):
+        block = jnp.transpose(tab[slot])
+        lane = lax.broadcasted_iota(jnp.int32, block.shape, 1)
+        return jnp.sum(jnp.where(lane == hosted, block, 0.0), axis=1, keepdims=True)
+
+    c0 = 0.7978845608028654
+    c1 = 0.044715
+
+    def work_in(slot):
+        column = gates(slot)
+        for part in range(2):
+            at = pl.ds(part * half, half)
+            x = xb[slot, at, :]
+            gate = column[part * half : (part + 1) * half]
+            g = jnp.dot(x, w_gate[...], preferred_element_type=f32)
+            u = jnp.dot(x, w_up[...], preferred_element_type=f32)
+            dz = (gate * dyb[slot, at, :].astype(f32)).astype(bf16)
+            dz_s[at, :] = dz
+            da = dot_nt(dz, w_down[...])
+            square = g * g
+            t = jnp.tanh(c0 * (g + c1 * square * g))
+            gelu = 0.5 * g * (1.0 + t)
+            slope = 0.5 * (1.0 + t) + 0.5 * g * (1.0 - t * t) * (c0 * (1.0 + 3.0 * c1 * square))
+            act_s[at, :] = (gelu * u).astype(bf16)
+            gate_s[at, :] = (da * u * slope).astype(bf16)
+            up_s[at, :] = (da * gelu).astype(bf16)
+        for part in range(3):
+            at = pl.ds(part * 512, 512)
+            x = xb[slot, :, at]
+            acc_gate[at, :] += dot_tn(x, gate_s[...])
+            acc_up[at, :] += dot_tn(x, up_s[...])
+            at = pl.ds(part * 256, 256)
+            acc_down[at, :] += dot_tn(act_s[:, at], dz_s[...])
+
+    def work_out(slot, dest):
+        column = gates(slot)
+        for part in range(2):
+            at = pl.ds(part * half, half)
+            gate = column[part * half : (part + 1) * half]
+            dx = dot_nt(gate_s[at, :], w_gate[...]) + dot_nt(up_s[at, :], w_up[...])
+            xb[dest, at, :] = dx.astype(bf16)
+            result = jnp.dot(act_s[at, :], w_down[...], preferred_element_type=f32)
+            dyb[dest, at, :] = (gate * result.astype(bf16).astype(f32)).astype(bf16)
+
+    def slot_at(step):
+        pair, odd = step // 2, lax.rem(step, 2)
+        last = pair // 3
+        return pair + 4 * (odd * (1 - last) + (1 - odd) * last)
+
+    @pl.loop(0, 8)
+    def _(step):
+        def at_step(number):
+            return pl.when(step == number)
+
+        @at_step(1)
+        def _():
+            start(2)
+            arrived(4)
+
+        @at_step(2)
+        def _():
+            arrived(1)
+            start(3)
+
+        @at_step(3)
+        def _():
+            arrived(5)
+
+        @at_step(4)
+        def _():
+            arrived(2)
+            start(5, 4)
+
+        @at_step(5)
+        def _():
+            arrived(6)
+
+        @at_step(6)
+        def _():
+            arrived(3)
+            start(6)
+            arrived(7)
+
+        slot = slot_at(step)
+        first_step = (8 - step) // 8
+        dest = (1 - first_step) * slot_at(step - 1 + first_step) + 8 * first_step
+        work_in(slot)
+
+        @at_step(3)
+        def _():
+            sent(3)
+
+        @at_step(5)
+        def _():
+            sent(5, 4)
+
+        work_out(slot, dest)
+
+        for number, (slot_now, slot_before) in enumerate(zip(SLOT_ORDER, (8,) + SLOT_ORDER)):
+
+            @at_step(number)
+            def _(slot_now=slot_now, slot_before=slot_before):
+                if slot_now < 4:
+                    keep_copy(slot_now, dyb.at[slot_before]).start()
+                else:
+                    for copy in part_copies(slot_now - 4, slot_before):
+                        copy.start()
+
+        @at_step(0)
+        def _():
+            own_grad.start()
+
+        @at_step(4)
+        def _():
+            part_copies(1, 1)[0].wait_recv()
+            xb[4] = (xb[4].astype(f32) + sib[0].astype(f32)).astype(bf16)
+            send_first.start()
+
+    part_copies(3, 6)[0].wait_recv()
+    xb[7] = (xb[7].astype(f32) + sib[2].astype(f32)).astype(bf16)
+    send_far.start()
+    w_gate[...] = acc_gate[...].astype(bf16)
+    w_up[...] = acc_up[...].astype(bf16)
+    w_down[...] = acc_down[...].astype(bf16)
+    stores = [
+        pltpu.make_async_copy(src, dst, store_sem.at[i])
+        for i, (src, dst) in enumerate(
+            ((w_gate, grad_gate_ref), (w_up, grad_up_ref), (w_down, grad_down_ref))
+        )
+    ]
+    for copy in stores:
+        copy.start()
+    part_copies(2, 2)[0].wait_recv()
+    send_far.wait_recv()
+    xb[5] = (xb[5].astype(f32) + sib[1].astype(f32) + far_in[...].astype(f32)).astype(bf16)
+    send_second.start()
+    sent(0, 1, 2, 6)
+    for j, slot_before in enumerate((0, 1, 2, 6)):
+        for k, copy in enumerate(part_copies(j, slot_before)):
+            copy.wait_send()
+            if k == 1 or j == 0:
+                copy.wait_recv()
+    for j, slot_before in enumerate((8, 4, 5, 7)):
+        keep_copy(j, dyb.at[slot_before]).wait()
+    own_grad.wait()
+    for copy in stores:
+        copy.wait()
+    send_first.wait()
+    send_far.wait_send()
+    send_second.wait()
+
+
+def moe_call(table, rows_in, grad_in, weight_gate, weight_up, weight_down):
+    f32, bf16 = jnp.float32, jnp.bfloat16
+    rows, width = rows_in.shape
+    hidden = weight_gate.shape[1]
+    anywhere = pl.BlockSpec(memory_space=pl.ANY)
+    chunk = jax.ShapeDtypeStruct((rows, width), bf16)
+    four = jax.ShapeDtypeStruct((4, rows, width), bf16)
+    wide = jax.ShapeDtypeStruct((width, hidden), bf16)
+    tall = jax.ShapeDtypeStruct((hidden, width), bf16)
+    dma = pltpu.SemaphoreType.DMA
+    return pl.pallas_call(
+        moe_kernel,
+        out_shape=(wide, wide, tall, four, four, chunk, chunk, chunk, chunk),
+        in_specs=[pl.BlockSpec(memory_space=pltpu.VMEM)] + [anywhere] * 5,
+        out_specs=(anywhere,) * 9,
+        scratch_shapes=[
+            pltpu.VMEM((9, rows, width), bf16),
+            pltpu.VMEM((9, rows, width), bf16),
+            pltpu.VMEM((8,) + table.shape, f32),
+            pltpu.VMEM((width, hidden), bf16),
+            pltpu.VMEM((width, hidden), bf16),
+            pltpu.VMEM((hidden, width), bf16),
+            pltpu.VMEM((width, hidden), f32),
+            pltpu.VMEM((width, hidden), f32),
+            pltpu.VMEM((hidden, width), f32),
+            pltpu.VMEM((rows, hidden), bf16),
+            pltpu.VMEM((rows, hidden), bf16),
+            pltpu.VMEM((rows, hidden), bf16),
+            pltpu.VMEM((rows, width), bf16),
+            pltpu.VMEM((3, rows, width), bf16),
+            pltpu.VMEM((rows, width), bf16),
+            dma((2, 7)),
+            dma((2, 7)),
+            dma((8,)),
+            dma((8,)),
+            dma((5,)),
+            dma((2, 4)),
+            dma((2, 4)),
+            dma((5,)),
+            dma((3,)),
+            dma((3,)),
+            dma((3,)),
+        ],
+        compiler_params=pltpu.CompilerParams(
+            collective_id=0, has_side_effects=True, vmem_limit_bytes=63 * 2**20
+        ),
+        cost_estimate=pl.CostEstimate(
+            flops=16 * 9 * rows * width * hidden, bytes_accessed=60 * 2**20, transcendentals=0
+        ),
+    )(table, rows_in, grad_in, weight_gate, weight_up, weight_down)
+
+
 def local_dense(
     tokens,
     segment_ids,
@@ -320,22 +642,13 @@
     def swap_core1(value, mask):
         return lax.ppermute(value, names, [(i, i ^ mask) for i in range(count) if i & bit_core])
 
-    def gather_group(chunk):
-        from_y = swap(chunk, bit_y)
-        from_z = swap(chunk, bit_z)
-        far = swap_mixed(jnp.where(on_core1, from_y, from_z), bit_y, bit_z)
-        mine = [chunk, from_y, from_z, far]
-        return mine + [swap(part, bit_core) for part in mine]
-
-    def reduce_group(parts):
-        own, to_y, to_z, far = [
-            parts[i].astype(f32) + swap(parts[4 + i], bit_core).astype(f32) for i in range(4)
+    def reduce_outputs(own_parts, sibling_parts):
+        own, to_first, to_second, far = [
+            own_parts[i].astype(f32) + sibling_parts[i].astype(f32) for i in range(4)
         ]
-        passed = swap_mixed(far.astype(bf16), bit_y, bit_z).astype(f32)
-        to_y = to_y + jnp.where(on_core1, passed, 0.0)
-        to_z = to_z + jnp.where(on_core1, 0.0, passed)
-        return own + swap(to_y.astype(bf16), bit_y).astype(f32) + swap(
-            to_z.astype(bf16), bit_z
+        to_second = to_second + swap_mixed(far.astype(bf16), bit_y, bit_z).astype(f32)
+        return own + swap_mixed(to_first.astype(bf16), bit_y, bit_z).astype(f32) + swap_mixed(
+            to_second.astype(bf16), bit_z, bit_y
         ).astype(f32)
 
     def fetch(weight):
@@ -351,7 +664,7 @@
         size = grad.shape[dim] // 2
         sent = lax.dynamic_slice_in_dim(grad, (1 - side) * size, size, dim).astype(bf16)
         kept = lax.dynamic_slice_in_dim(grad, side * size, size, dim)
-        half = kept + swap(sent, bit_x).astype(f32)
+        half = kept.astype(f32) + swap(sent, bit_x).astype(f32)
         foreign = swap_core1(half.astype(bf16), bit_far).astype(f32)
         base = jnp.where(on_core1, foreign, half)
         size = size // 2
@@ -372,7 +685,6 @@
             block = kept.astype(f32) + swap(sent.astype(bf16), mask).astype(f32)
         return block.reshape(rows // count, columns)
 
-    cotangent_parts = gather_group(cotangent)
     weight_gate = fetch(expert_gate[0])
     weight_up = fetch(expert_up[0])
     weight_down = fetch(expert_down[0])
@@ -384,10 +696,6 @@
         ),
         axis=1,
     )
-    tables = jnp.stack(gather_group(table.T))
-    hosted = lax.axis_index("ep") ^ (bit_far * core)
-    gate_column = lax.dynamic_index_in_dim(tables, hosted, 1, keepdims=False).reshape(-1)[:, None]
-
     query_heads = query_weight.shape[1] // HEAD_SIZE
     key_heads = key_matrix.shape[1] // HEAD_SIZE
     q_per_kv = query_heads // key_heads
@@ -440,31 +748,17 @@
     normed_second = mixed * scale_second
     h_second = (normed_second * ffn_gain).astype(jnp.bfloat16)
 
-    rows_in = jnp.concatenate(gather_group(h_second), axis=0)
-    grad_in = jnp.concatenate(cotangent_parts, axis=0)
-    gate_val = jnp.dot(rows_in, weight_gate, preferred_element_type=f32)
-    up_val = jnp.dot(rows_in, weight_up, preferred_element_type=f32)
-    act, act_back = jax.vjp(glu_value, gate_val, up_val)
-    act_low = act.astype(bf16)
-    result = jnp.dot(act_low, weight_down, preferred_element_type=f32).astype(bf16)
-    weighted = (gate_column * result.astype(f32)).astype(bf16)
-    slot_grads = (gate_column * grad_in.astype(f32)).astype(bf16)
-    act_grad = jnp.einsum("td,fd->tf", slot_grads, weight_down, preferred_element_type=f32)
-    gate_grad_val, up_grad_val = act_back(act_grad)
-    gate_low = gate_grad_val.astype(bf16)
-    up_low = up_grad_val.astype(bf16)
-    rows_grad = jnp.einsum("tf,df->td", gate_low, weight_gate, preferred_element_type=f32)
-    rows_grad = rows_grad + jnp.einsum("tf,df->td", up_low, weight_up, preferred_element_type=f32)
-    rows_grad = rows_grad.astype(bf16)
-    second_grad = reduce_group(
-        [rows_grad[i * length_total : (i + 1) * length_total] for i in range(8)]
-    )
-    down_part = jnp.einsum("tf,td->fd", act_low, slot_grads, preferred_element_type=f32)
-    gate_part = jnp.einsum("td,tf->df", rows_in, gate_low, preferred_element_type=f32)
-    up_part = jnp.einsum("td,tf->df", rows_in, up_low, preferred_element_type=f32)
+    (
+        gate_part,
+        up_part,
+        down_part,
+        out_own,
+        out_sib,
+        *second_parts,
+    ) = moe_call(table.T, h_second, cotangent, weight_gate, weight_up, weight_down)
+    second_grad = sum(part.astype(f32) for part in second_parts)
     expert_sums = (give(gate_part, 0)[None], give(up_part, 0)[None], give(down_part, 1)[None])
-    combined = reduce_group([weighted[i * length_total : (i + 1) * length_total] for i in range(8)])
-    layer_out = (mixed + combined).astype(bf16)
+    layer_out = (mixed + reduce_outputs(out_own, out_sib)).astype(bf16)
     grad_out = cotangent.astype(f32)
     ffn_gain_part = jnp.sum(second_grad * normed_second, axis=0)
     normed_grad = second_grad * ffn_gain

time: 742 us -> 663 us (0.89)
  Pallas kernels: 0 us -> 242 us
  matrix products: 230 us -> 69.2 us
  starting transfers between devices: 144 us -> 66.4 us
  waiting for transfers between devices: 171 us -> 128 us
  local copies, waits for them, and re-layouts: 87.5 us -> 53.1 us
    pallas_call x0 -> x1, Pallas kernels: none -> 242 us  [moe_call(): pl.pallas_call(moe_kernel, out_shape=(wide, wide, tall, four, four, chunk...]
    dot_general x9 -> x0, matrix products: 160 us -> none  [the longest x1 29.9 us: local_dense(): gate_val = jnp.dot(rows_in, weight_gate, preferred_element_type=f32)]
    ppermute x46 -> x16, starting transfers between devices: 128 us -> 50.3 us  [swap(): return lax.ppermute(value, names, [(i, i ^ mask) for i in range(count)])]
    ppermute x46 -> x16, waiting for transfers between devices: 145 us -> 83.5 us  [swap(): return lax.ppermute(value, names, [(i, i ^ mask) for i in range(count)])]
    unnamed x200 -> x172, local copies, waits for them, and re-layouts: 45.5 us -> 20 us
    ppermute x5 -> x3, waiting for transfers between devices: 25.1 us -> 44.2 us  [swap_mixed(): lax.ppermute(value, names, [(i, i ^ (mask1 if i & bit_core else mask0)) f...]
    slice x2 -> x0, local copies, waits for them, and re-layouts: 7.75 us -> none  [the longest x1 4.93 us: local_dense(): rows_grad[i * length_total:(i + 1) * length_total]]
    convert_element_type x4 -> x3, other arithmetic: 17.2 us -> 12.9 us  [the longest x1 5.47 us: reduce_outputs(): to_first.astype(bf16)]
  transfers between devices with their start and end apart: 60 -> 28, of which waited for: 11 -> 8; matrix products, arithmetic and copies ran while one was open for 45% -> 29% of each run, Pallas kernels for 0% -> 0%
where the time goes in v2:
time: 663 us; the launch traced here: 659 us
  Pallas kernels  242 us (37%)
  waiting for transfers between devices  128 us (19%)
  other arithmetic  97.5 us (15%)
  matrix products  69.2 us (10%)
  starting transfers between devices  66.4 us (10%)
  local copies, waits for them, and re-layouts  53.1 us (8%)
    pallas_call x1, Pallas kernels, moe_call(): pl.pallas_call(moe_kernel, out_shape=(wide, wide, tall, four, four, chunk...  242 us
    ppermute x16, waiting for transfers between devices, swap(): return lax.ppermute(value, names, [(i, i ^ mask) for i in range(count)])  83.5 us
    ppermute x16, starting transfers between devices, swap(): return lax.ppermute(value, names, [(i, i ^ mask) for i in range(count)])  50.3 us
    ppermute x3, waiting for transfers between devices, swap_mixed(): lax.ppermute(value, names, [(i, i ^ (mask1 if i & bit_core else mask0)) f...  44.2 us
    unnamed x172, local copies, waits for them, and re-layouts  20 us
  transfers between devices with their start and end apart: 28, of which 8 were waited for; matrix products, arithmetic and copies ran while one was open for 29% of the time, Pallas kernels for 0%

profile of v2, /device:TPU:0, one launch (start us, length us, event | category | flops | bytes accessed | tf_op | source)
XLA Modules:
  0.0 658.5 jit_solution(310143495184840490)
XLA Ops:
  21.0 4.9 fusion.62
  34.2 3.4 fusion.13
  42.4 3.8 fusion.34
  47.5 6.9 %multiply_reduce_fusion.2 = (f32[512]{0:T(512)S(1)}, f32[512,1536]{1,0:T(8,128)}) fusion(bf16[512,1536]{0,1:T(8,128)(2,1)S(1)} %bitcast.177, bf16[1536,1536]{1,0:T(8,128)(2,1)} %param.23, bf16[512,1536]{1,0:T(8,128)(2,1)S(1)} %copy-done.9), kind=kOutput, calls=%fused_computation.52 | convolution fusion | flops 2419064320 | bytes 11012096 | tf_op jit(solution)/shard_map/dot_general | solution.py:746
  55.7 3.4 multiply_convert_fusion.h_ref
  70.9 242.4 %shard_map.221 = (bf16[1536,768]{1,0:T(8,128)(2,1)}, bf16[1536,768]{1,0:T(8,128)(2,1)}, bf16[768,1536]{1,0:T(8,128)(2,1)}, bf16[4,512,1536]{2,1,0:T(8,128)(2,1)}...) custom-call(f32[8,512]{1,0:T(8,128)} %bitcast.174, ...), custom_call_target="tpu_custom_call" | custom-call | flops 86973087744 | bytes 62914560 | tf_op jit(solution)/shard_map/pallas_call | solution.py:564
  313.3 5.5 fusion.35
  323.4 16.1 %collective-permute-done.7 = bf16[512,1536]{1,0:T(8,128)(2,1)} collective-permute-done((bf16[512,1536]{1,0:T(8,128)(2,1)}, bf16[512,1536]{1,0:T(8,128)(2,1)}, u32[]{:S(2)}, u32[]{:S(2)}) %collective-permute-start.7) | collective-permute-done | bytes 1572896 | tf_op jit(solution)/shard_map/ppermute | solution.py:638
  339.5 4.1 fusion.21
  345.4 4.8 multiply_reduce_fusion
  357.6 8.6 %collective-permute-done.6 = bf16[512,1536]{1,0:T(8,128)(2,1)} collective-permute-done((bf16[512,1536]{1,0:T(8,128)(2,1)}, bf16[512,1536]{1,0:T(8,128)(2,1)}, u32[]{:S(2)}, u32[]{:S(2)}) %collective-permute-start.6) | collective-permute-done | bytes 1572896 | tf_op jit(solution)/shard_map/ppermute | solution.py:638
  366.3 19.5 %collective-permute-done.8 = bf16[512,1536]{1,0:T(8,128)(2,1)} collective-permute-done((bf16[512,1536]{1,0:T(8,128)(2,1)}, bf16[512,1536]{1,0:T(8,128)(2,1)}, u32[]{:S(2)}, u32[]{:S(2)}) %collective-permute-start.8) | collective-permute-done | bytes 1572896 | tf_op jit(solution)/shard_map/ppermute | solution.py:638
  385.8 5.8 convert_bitcast_fusion
  393.3 3.8 convolution_convert_fusion
  398.9 8.7 %fusion.42 = bf16[2,128,512]{2,1,0:T(8,128)(2,1)} fusion(bf16[512,2,6,128]{0,3,2,1:T(8,128)(2,1)S(1)} %bitcast.160, f32[2,6,512]{2,1,0:T(8,128)S(1)} %copy-done.57, f32[2,512,512,6]{2,1,3,0:T(8,128)} %copy-done.1, pred[512,512]{0,1:T(8,128)(4,1)S(1)} %copy-done.12), kind=kOutput, calls=%fused_computation.90 | convolution fusion | flops 818020352 | bytes 14704640 | tf_op jit(solution)/shard_map/kgts,tkgd->skd/dot_general | solution.py:779
  407.6 9.7 %fusion = (f32[2,6,512]{2,1,0:T(8,128)S(1)}, f32[2,512,512,6]{2,1,3,0:T(8,128)}) fusion(f32[2,6,512]{2,1,0:T(8,128)S(1)} %copy-done.57, f32[2,512,512,6]{2,1,3,0:T(8,128)} %copy-done.1, pred[512,512]{0,1:T(8,128)(4,1)S(1)} %copy-done.12, bf16[512,2,128,1]{0,2,3,1:T(8,128)(2,1)S(1)} %bitcast.170, bf16[512,2,6,128]{0,3,2,1:T(8,128)(2,1)S(1)} %bitcast.161), kind=kOutput, calls=%fused_computation.4 | convolution fusion | flops 821028864 | bytes 27312128 | tf_op jit(solution)/shard_map/tkgd,skd->kgts/dot_general | solution.py:782
  417.3 7.5 %fusion.2 = bf16[2,6,512,512]{2,3,1,0:T(8,128)(2,1)S(1)} fusion(f32[2,512,512,6]{2,1,3,0:T(8,128)} %get-tuple-element.65, f32[2,6,512]{2,1,0:T(8,128)S(1)} %get-tuple-element.64, f32[2,6,512]{2,1,0:T(8,128)S(1)} %copy-done.57, f32[2,512,512,6]{2,1,3,0:T(8,128)S(1)} %bitcast.148, pred[512,512]{0,1:T(8,128)(4,1)S(1)} %copy-done.12), kind=kLoop, calls=%fused_computation.6 | loop fusion | flops 18874368 | bytes 31768576 | tf_op jit(solution)/shard_map/convert_element_type | solution.py:786
  433.2 4.7 fusion.69
  439.4 3.1 fusion.19
  442.5 8.0 %fusion.28 = f32[1536,2048]{1,0:T(8,128)} fusion(bf16[512,256]{0,1:T(8,128)(2,1)S(1)} %bitcast.172, bf16[512,256]{0,1:T(8,128)(2,1)S(1)} %bitcast.167, bf16[512,1536]{0,1:T(8,128)(2,1)S(1)} %bitcast.164, bf16[512,1536]{1,0:T(8,128)(2,1)S(1)} %copy-done.10, f32[1536]{0:T(1024)S(1)} %copy-done.68, f32[512]{0:T(512)S(1)} %copy-done.70), kind=kOutput, calls=%fused_computation.68 | convolution fusion | flops 3230662656 | bytes 16261120 | tf_op jit(solution)/shard_map/td,ti->di/dot_general | solution.py:808
  453.2 4.5 fusion.70
  457.8 3.6 copy-done.27
  463.4 10.7 %select_maximum_fusion = f32[1536,2176]{1,0:T(8,128)} fusion(f32[1536,4]{1,0:T(8,128)S(1)} %copy.111, f32[1536,2048]{1,0:T(8,128)} %fusion.28), kind=kLoop, calls=%fused_computation | loop fusion | flops 10027008 | bytes 25976832 | tf_op jit(solution)/shard_map/concatenate | solution.py:828
  474.1 5.2 dynamic-slice_convert_fusion
  500.8 29.6 %collective-permute-start.24 = (bf16[384,768]{1,0:T(8,128)(2,1)}, bf16[384,768]{1,0:T(8,128)(2,1)}, u32[]{:S(2)}, u32[]{:S(2)}) collective-permute-start(bf16[384,768]{1,0:T(8,128)(2,1)} %dynamic-slice_convert_fusion.6), channel_id=1, source_target_pairs={{0,8},{1,9},{2,10},{3,11},{4,12},{5,13},{6,14},{7,15},{8,0},{9,1},... | collective-permute-start | bytes 1769480 | tf_op jit(solution)/shard_map/ppermute | solution.py:635
  534.8 8.2 %collective-permute-start.21 = (bf16[384,768]{1,0:T(8,128)(2,1)}, bf16[384,768]{1,0:T(8,128)(2,1)}, u32[]{:S(2)}, u32[]{:S(2)}) collective-permute-start(bf16[384,768]{1,0:T(8,128)(2,1)} %dynamic-slice_convert_fusion.7), channel_id=1, source_target_pairs={{0,8},{1,9},{2,10},{3,11},{4,12},{5,13},{6,14},{7,15},{8,0},{9,1},... | collective-permute-start | bytes 1769480 | tf_op jit(solution)/shard_map/ppermute | solution.py:635
  543.1 3.8 convert_add_fusion.2
  561.4 15.8 %collective-permute-done.15 = bf16[1,1,2,2,2,48,1536]{6,5,4,3,2,1,0:T(8,128)(2,1)} collective-permute-done((bf16[1,1,2,2,2,48,1536]{6,5,4,3,2,1,0:T(8,128)(2,1)}, bf16[1,1,2,2,2,48,1536]{6,5,4,3,2,1,0:T(8,128)(2,1)}, u32[]{:S(2)}, u32[]{:S(2)}) %collective-permute-start.15) | collective-permute-done | bytes 1179680 | tf_op jit(solution)/shard_map/ppermute | solution.py:635
  579.2 32.9 %collective-permute-done.10 = bf16[1,1,2,2,2,48,2176]{6,5,4,3,2,1,0:T(8,128)(2,1)S(1)} collective-permute-done((bf16[1,1,2,2,2,48,2176]{6,5,4,3,2,1,0:T(8,128)(2,1)S(1)}, bf16[1,1,2,2,2,48,2176]{6,5,4,3,2,1,0:T(8,128)(2,1)S(1)}, u32[]{:S(2)}, u32[]{:S(2)}) %collective-permute-start.10) | collective-permute-done | bytes 1671200 | tf_op jit(solution)/shard_map/ppermute | solution.py:635
  617.8 14.6 %collective-permute-done.11 = bf16[1,1,2,2,1,48,2176]{6,5,4,3,2,1,0:T(8,128)(2,1)S(1)} collective-permute-done((bf16[1,1,2,2,1,48,2176]{6,5,4,3,2,1,0:T(8,128)(2,1)S(1)}, bf16[1,1,2,2,1,48,2176]{6,5,4,3,2,1,0:T(8,128)(2,1)S(1)}, u32[]{:S(2)}, u32[]{:S(2)}) %collective-permute-start.11) | collective-permute-done | bytes 835616 | tf_op jit(solution)/shard_map/ppermute | solution.py:635
  635.0 10.6 %collective-permute-done.12 = bf16[1,1,2,1,1,48,2176]{6,5,4,3,2,1,0:T(8,128)(2,1)S(1)} collective-permute-done((bf16[1,1,2,1,1,48,2176]{6,5,4,3,2,1,0:T(8,128)(2,1)S(1)}, bf16[1,1,2,1,1,48,2176]{6,5,4,3,2,1,0:T(8,128)(2,1)S(1)}, u32[]{:S(2)}, u32[]{:S(2)}) %collective-permute-start.12) | collective-permute-done | bytes 417824 | tf_op jit(solution)/shard_map/ppermute | solution.py:635
  646.6 9.5 %collective-permute-done.13 = bf16[1,1,1,1,1,48,2176]{6,5,4,3,2,1,0:T(8,128)(2,1)S(1)} collective-permute-done((bf16[1,1,1,1,1,48,2176]{6,5,4,3,2,1,0:T(8,128)(2,1)S(1)}, bf16[1,1,1,1,1,48,2176]{6,5,4,3,2,1,0:T(8,128)(2,1)S(1)}, u32[]{:S(2)}, u32[]{:S(2)}) %collective-permute-start.13) | collective-permute-done | bytes 208928 | tf_op jit(solution)/shard_map/ppermute | solution.py:635
  (305 shorter events, 132.6 us)
Async XLA Ops:
  3.2 43.0 %collective-permute-start.2 = (bf16[768,768]{1,0:T(8,128)(2,1)}, bf16[768,768]{1,0:T(8,128)(2,1)}, u32[]{:S(2)}, u32[]{:S(2)}) collective-permute-start(bf16[768,768]{1,0:T(8,128)(2,1)} %dynamic-slice_bitcast_fusion.1), channel_id=1, source_target_pairs={{8,12},{9,13},{10,14},{11,15},{12,8},{13,9},{14,10},{15,11},{24,28... | collective-permute-start | bytes 3538952 | tf_op jit(solution)/shard_map/ppermute | solution.py:643
  6.1 53.0 %collective-permute-start = (bf16[768,768]{1,0:T(8,128)(2,1)}, bf16[768,768]{1,0:T(8,128)(2,1)}, u32[]{:S(2)}, u32[]{:S(2)}) collective-permute-start(bf16[768,768]{1,0:T(8,128)(2,1)} %dynamic-slice_bitcast_fusion.2), channel_id=1, source_target_pairs={{8,12},{9,13},{10,14},{11,15},{12,8},{13,9},{14,10},{15,11},{24,28... | collective-permute-start | bytes 3538952 | tf_op jit(solution)/shard_map/ppermute | solution.py:643
  10.3 44.1 %collective-permute-start.4 = (bf16[384,1536]{1,0:T(8,128)(2,1)}, bf16[384,1536]{1,0:T(8,128)(2,1)}, u32[]{:S(2)}, u32[]{:S(2)}) collective-permute-start(bf16[384,1536]{1,0:T(8,128)(2,1)} %dynamic-slice_bitcast_fusion), channel_id=1, source_target_pairs={{8,12},{9,13},{10,14},{11,15},{12,8},{13,9},{14,10},{15,11},{24,28... | collective-permute-start | bytes 3538952 | tf_op jit(solution)/shard_map/ppermute | solution.py:643
  46.3 13.5 %collective-permute-start.3 = (bf16[768,768]{1,0:T(8,128)(2,1)}, bf16[768,768]{1,0:T(8,128)(2,1)S(1)}, u32[]{:S(2)}, u32[]{:S(2)}) collective-permute-start(bf16[768,768]{1,0:T(8,128)(2,1)} %collective-permute-done.2), channel_id=1, source_target_pairs={{8,24},{9,25},{10,26},{11,27},{12,28},{13,29},{14,30},{15,31},{24,... | collective-permute-start | bytes 3538952 | tf_op jit(solution)/shard_map/ppermute | solution.py:643
  54.3 6.9 %collective-permute-start.5 = (bf16[384,1536]{1,0:T(8,128)(2,1)}, bf16[384,1536]{1,0:T(8,128)(2,1)S(1)}, u32[]{:S(2)}, u32[]{:S(2)}) collective-permute-start(bf16[384,1536]{1,0:T(8,128)(2,1)} %collective-permute-done.4), channel_id=1, source_target_pairs={{8,24},{9,25},{10,26},{11,27},{12,28},{13,29},{14,30},{15,31},{24,... | collective-permute-start | bytes 3538952 | tf_op jit(solution)/shard_map/ppermute | solution.py:643
  55.7 289.6 %copy-start.64 = (f32[512]{0:T(512)}, f32[512]{0:T(512)S(1)}, u32[]{:S(2)}) copy-start(f32[512]{0:T(512)S(1)} %add_rsqrt_fusion) | copy-start | bytes 6148
  59.1 6.2 collective-permute-start.1
  318.8 20.7 %collective-permute-start.7 = (bf16[512,1536]{1,0:T(8,128)(2,1)}, bf16[512,1536]{1,0:T(8,128)(2,1)}, u32[]{:S(2)}, u32[]{:S(2)}) collective-permute-start(bf16[512,1536]{1,0:T(8,128)(2,1)} %get-tuple-element.38), channel_id=1, source_target_pairs={{0,1},{1,0},{2,3},{3,2},{4,5},{5,4},{6,7},{7,6},{8,10},{9,11},{10,... | collective-permute-start | bytes 4718600 | tf_op jit(solution)/shard_map/ppermute | solution.py:638
  321.4 33.1 %collective-permute-start.25 = (bf16[768,768]{1,0:T(8,128)(2,1)}, bf16[768,768]{1,0:T(8,128)(2,1)S(1)}, u32[]{:S(2)}, u32[]{:S(2)}) collective-permute-start(bf16[768,768]{1,0:T(8,128)(2,1)} %constant_dynamic-slice_fusion), channel_id=1, source_target_pairs={{0,16},{1,17},{2,18},{3,19},{4,20},{5,21},{6,22},{7,23},{8,24},{9,... | collective-permute-start | bytes 3538952 | tf_op jit(solution)/shard_map/ppermute | solution.py:635
  322.9 43.4 %collective-permute-start.6 = (bf16[512,1536]{1,0:T(8,128)(2,1)}, bf16[512,1536]{1,0:T(8,128)(2,1)}, u32[]{:S(2)}, u32[]{:S(2)}) collective-permute-start(bf16[512,1536]{1,0:T(8,128)(2,1)} %get-tuple-element.37), channel_id=1, source_target_pairs={{0,1},{1,0},{2,3},{3,2},{4,5},{5,4},{6,7},{7,6},{8,10},{9,11},{10,... | collective-permute-start | bytes 4718600 | tf_op jit(solution)/shard_map/ppermute | solution.py:638
  343.6 42.1 %collective-permute-start.8 = (bf16[512,1536]{1,0:T(8,128)(2,1)}, bf16[512,1536]{1,0:T(8,128)(2,1)}, u32[]{:S(2)}, u32[]{:S(2)}) collective-permute-start(bf16[512,1536]{1,0:T(8,128)(2,1)} %fusion.21), channel_id=1, source_target_pairs={{0,2},{1,3},{2,0},{3,1},{4,6},{5,7},{6,4},{7,5},{8,9},{9,8},{10,11... | collective-permute-start | bytes 4718600 | tf_op jit(solution)/shard_map/ppermute | solution.py:638
  351.4 128.4 %collective-permute-start.22 = (bf16[768,768]{1,0:T(8,128)(2,1)}, bf16[768,768]{1,0:T(8,128)(2,1)}, u32[]{:S(2)}, u32[]{:S(2)}) collective-permute-start(bf16[768,768]{1,0:T(8,128)(2,1)} %constant_dynamic-slice_fusion.1), channel_id=1, source_target_pairs={{0,16},{1,17},{2,18},{3,19},{4,20},{5,21},{6,22},{7,23},{8,24},{9,... | collective-permute-start | bytes 3538952 | tf_op jit(solution)/shard_map/ppermute | solution.py:635
  354.0 130.4 %collective-permute-start.19 = (bf16[768,768]{1,0:T(8,128)(2,1)}, bf16[768,768]{1,0:T(8,128)(2,1)}, u32[]{:S(2)}, u32[]{:S(2)}) collective-permute-start(bf16[768,768]{1,0:T(8,128)(2,1)} %constant_dynamic-slice_fusion.2), channel_id=1, source_target_pairs={{0,16},{1,17},{2,18},{3,19},{4,20},{5,21},{6,22},{7,23},{8,24},{9,... | collective-permute-start | bytes 3538952 | tf_op jit(solution)/shard_map/ppermute | solution.py:635
  355.8 132.8 %collective-permute-start.26 = (bf16[768,768]{1,0:T(8,128)(2,1)}, bf16[768,768]{1,0:T(8,128)(2,1)}, u32[]{:S(2)}, u32[]{:S(2)}) collective-permute-start(bf16[768,768]{1,0:T(8,128)(2,1)} %fusion.27), channel_id=1, source_target_pairs={{8,12},{9,13},{10,14},{11,15},{12,8},{13,9},{14,10},{15,11},{24,28... | collective-permute-start | bytes 3538952 | tf_op jit(solution)/shard_map/ppermute | solution.py:643
  463.1 80.0 %collective-permute-start.14 = (bf16[2,1,2,2,2,48,1536]{6,5,4,3,2,1,0:T(8,128)(2,1)}, bf16[2,1,2,2,2,48,1536]{6,5,4,3,2,1,0:T(8,128)(2,1)}, u32[]{:S(2)}, u32[]{:S(2)}) collective-permute-start(bf16[2,1,2,2,2,48,1536]{6,5,4,3,2,1,0:T(8,128)(2,1)} %dynamic-slice_convert_fusion.1), channel_id=1, source_target_pairs={{0,8},{1,9},{2,10},{3,11},{4,12},{5,13},{6,14},{7,15},{8,0},{9,1},... | collective-permute-start | bytes 7077896 | tf_op jit(solution)/shard_map/ppermute | solution.py:635
  479.3 70.3 %collective-permute-start.9 = (bf16[2,1,2,2,2,48,2176]{6,5,4,3,2,1,0:T(8,128)(2,1)}, bf16[2,1,2,2,2,48,2176]{6,5,4,3,2,1,0:T(8,128)(2,1)}, u32[]{:S(2)}, u32[]{:S(2)}) collective-permute-start(bf16[2,1,2,2,2,48,2176]{6,5,4,3,2,1,0:T(8,128)(2,1)} %dynamic-slice_convert_fusion), channel_id=1, source_target_pairs={{0,8},{1,9},{2,10},{3,11},{4,12},{5,13},{6,14},{7,15},{8,0},{9,1},... | collective-permute-start | bytes 10027016 | tf_op jit(solution)/shard_map/ppermute | solution.py:635
  482.6 13.8 %collective-permute-start.23 = (bf16[768,768]{1,0:T(8,128)(2,1)}, bf16[768,768]{1,0:T(8,128)(2,1)}, u32[]{:S(2)}, u32[]{:S(2)}) collective-permute-start(bf16[768,768]{1,0:T(8,128)(2,1)} %fusion.26), channel_id=1, source_target_pairs={{8,12},{9,13},{10,14},{11,15},{12,8},{13,9},{14,10},{15,11},{24,28... | collective-permute-start | bytes 3538952 | tf_op jit(solution)/shard_map/ppermute | solution.py:643
  486.9 43.5 %collective-permute-start.20 = (bf16[768,768]{1,0:T(8,128)(2,1)}, bf16[768,768]{1,0:T(8,128)(2,1)}, u32[]{:S(2)}, u32[]{:S(2)}) collective-permute-start(bf16[768,768]{1,0:T(8,128)(2,1)} %fusion.25), channel_id=1, source_target_pairs={{8,12},{9,13},{10,14},{11,15},{12,8},{13,9},{14,10},{15,11},{24,28... | collective-permute-start | bytes 3538952 | tf_op jit(solution)/shard_map/ppermute | solution.py:643
  488.6 61.0 %slice-start.3 = ((s8[13369344]{0:T(1024)(128)(4,1)}), s8[4194304]{0:T(1024)(128)(4,1)S(1)}, s32[]{:S(2)}) async-start(s8[13369344]{0:T(1024)(128)(4,1)} %bitcast.150), calls=%async_computation.3 | async-start | bytes 8388608
  493.5 56.1 %slice-start.4 = ((s8[13369344]{0:T(1024)(128)(4,1)}), s8[4194304]{0:T(1024)(128)(4,1)S(1)}, s32[]{:S(2)}) async-start(s8[13369344]{0:T(1024)(128)(4,1)} %bitcast.150), calls=%async_computation.4 | async-start | bytes 8388608
  493.5 60.4 %collective-permute-start.27 = (bf16[768,384]{1,0:T(8,128)(2,1)}, bf16[768,384]{1,0:T(8,128)(2,1)}, u32[]{:S(2)}, u32[]{:S(2)}) collective-permute-start(bf16[768,384]{1,0:T(8,128)(2,1)} %dynamic-slice_convert_fusion.5), channel_id=1, source_target_pairs={{0,8},{1,9},{2,10},{3,11},{4,12},{5,13},{6,14},{7,15},{8,0},{9,1},... | collective-permute-start | bytes 1769480 | tf_op jit(solution)/shard_map/ppermute | solution.py:635
  500.8 48.8 %slice-start.5 = ((s8[13369344]{0:T(1024)(128)(4,1)}), s8[4194304]{0:T(1024)(128)(4,1)S(1)}, s32[]{:S(2)}) async-start(s8[13369344]{0:T(1024)(128)(4,1)} %bitcast.150), calls=%async_computation.5 | async-start | bytes 8388608
  500.8 56.2 %collective-permute-start.24 = (bf16[384,768]{1,0:T(8,128)(2,1)}, bf16[384,768]{1,0:T(8,128)(2,1)}, u32[]{:S(2)}, u32[]{:S(2)}) collective-permute-start(bf16[384,768]{1,0:T(8,128)(2,1)} %dynamic-slice_convert_fusion.6), channel_id=1, source_target_pairs={{0,8},{1,9},{2,10},{3,11},{4,12},{5,13},{6,14},{7,15},{8,0},{9,1},... | collective-permute-start | bytes 1769480 | tf_op jit(solution)/shard_map/ppermute | solution.py:635
  534.8 24.4 %collective-permute-start.21 = (bf16[384,768]{1,0:T(8,128)(2,1)}, bf16[384,768]{1,0:T(8,128)(2,1)}, u32[]{:S(2)}, u32[]{:S(2)}) collective-permute-start(bf16[384,768]{1,0:T(8,128)(2,1)} %dynamic-slice_convert_fusion.7), channel_id=1, source_target_pairs={{0,8},{1,9},{2,10},{3,11},{4,12},{5,13},{6,14},{7,15},{8,0},{9,1},... | collective-permute-start | bytes 1769480 | tf_op jit(solution)/shard_map/ppermute | solution.py:635
  548.1 29.1 %collective-permute-start.15 = (bf16[1,1,2,2,2,48,1536]{6,5,4,3,2,1,0:T(8,128)(2,1)}, bf16[1,1,2,2,2,48,1536]{6,5,4,3,2,1,0:T(8,128)(2,1)}, u32[]{:S(2)}, u32[]{:S(2)}) collective-permute-start(bf16[1,1,2,2,2,48,1536]{6,5,4,3,2,1,0:T(8,128)(2,1)} %dynamic-slice_convert_fusion.3), channel_id=1, source_target_pairs={{0,16},{1,17},{2,18},{3,19},{4,20},{5,21},{6,22},{7,23},{8,24},{9,... | collective-permute-start | bytes 3538952 | tf_op jit(solution)/shard_map/ppermute | solution.py:635
  552.6 59.4 %collective-permute-start.10 = (bf16[1,1,2,2,2,48,2176]{6,5,4,3,2,1,0:T(8,128)(2,1)S(1)}, bf16[1,1,2,2,2,48,2176]{6,5,4,3,2,1,0:T(8,128)(2,1)S(1)}, u32[]{:S(2)}, u32[]{:S(2)}) collective-permute-start(bf16[1,1,2,2,2,48,2176]{6,5,4,3,2,1,0:T(8,128)(2,1)S(1)} %dynamic-slice_convert_fusion.2), channel_id=1, source_target_pairs={{0,16},{1,17},{2,18},{3,19},{4,20},{5,21},{6,22},{7,23},{8,24},{9,... | collective-permute-start | bytes 5013512 | tf_op jit(solution)/shard_map/ppermute | solution.py:635
  579.0 38.5 %collective-permute-start.16 = (bf16[1,1,2,2,1,48,1536]{6,5,4,3,2,1,0:T(8,128)(2,1)S(1)}, bf16[1,1,2,2,1,48,1536]{6,5,4,3,2,1,0:T(8,128)(2,1)S(1)}, u32[]{:S(2)}, u32[]{:S(2)}) collective-permute-start(bf16[1,1,2,2,1,48,1536]{6,5,4,3,2,1,0:T(8,128)(2,1)S(1)} %dynamic-slice_convert_fusion.8), channel_id=1, source_target_pairs={{0,1},{1,0},{2,3},{3,2},{4,5},{5,4},{6,7},{7,6},{8,9},{9,8},{10,11... | collective-permute-start | bytes 1769480 | tf_op jit(solution)/shard_map/ppermute | solution.py:635
  612.5 19.8 %collective-permute-start.11 = (bf16[1,1,2,2,1,48,2176]{6,5,4,3,2,1,0:T(8,128)(2,1)S(1)}, bf16[1,1,2,2,1,48,2176]{6,5,4,3,2,1,0:T(8,128)(2,1)S(1)}, u32[]{:S(2)}, u32[]{:S(2)}) collective-permute-start(bf16[1,1,2,2,1,48,2176]{6,5,4,3,2,1,0:T(8,128)(2,1)S(1)} %dynamic-slice_convert_fusion.4), channel_id=1, source_target_pairs={{0,1},{1,0},{2,3},{3,2},{4,5},{5,4},{6,7},{7,6},{8,9},{9,8},{10,11... | collective-permute-start | bytes 2506760 | tf_op jit(solution)/shard_map/ppermute | solution.py:635
  617.7 15.0 %collective-permute-start.17 = (bf16[1,1,2,1,1,48,1536]{6,5,4,3,2,1,0:T(8,128)(2,1)S(1)}, bf16[1,1,2,1,1,48,1536]{6,5,4,3,2,1,0:T(8,128)(2,1)S(1)}, u32[]{:S(2)}, u32[]{:S(2)}) collective-permute-start(bf16[1,1,2,1,1,48,1536]{6,5,4,3,2,1,0:T(8,128)(2,1)S(1)} %dynamic-slice_convert_fusion.10), channel_id=1, source_target_pairs={{0,2},{1,3},{2,0},{3,1},{4,6},{5,7},{6,4},{7,5},{8,10},{9,11},{10,... | collective-permute-start | bytes 884744 | tf_op jit(solution)/shard_map/ppermute | solution.py:635
  632.6 13.1 %collective-permute-start.12 = (bf16[1,1,2,1,1,48,2176]{6,5,4,3,2,1,0:T(8,128)(2,1)S(1)}, bf16[1,1,2,1,1,48,2176]{6,5,4,3,2,1,0:T(8,128)(2,1)S(1)}, u32[]{:S(2)}, u32[]{:S(2)}) collective-permute-start(bf16[1,1,2,1,1,48,2176]{6,5,4,3,2,1,0:T(8,128)(2,1)S(1)} %dynamic-slice_convert_fusion.9), channel_id=1, source_target_pairs={{0,2},{1,3},{2,0},{3,1},{4,6},{5,7},{6,4},{7,5},{8,10},{9,11},{10,... | collective-permute-start | bytes 1253384 | tf_op jit(solution)/shard_map/ppermute | solution.py:635
  632.7 13.1 %collective-permute-start.18 = (bf16[1,1,1,1,1,48,1536]{6,5,4,3,2,1,0:T(8,128)(2,1)S(1)}, bf16[1,1,1,1,1,48,1536]{6,5,4,3,2,1,0:T(8,128)(2,1)S(1)}, u32[]{:S(2)}, u32[]{:S(2)}) collective-permute-start(bf16[1,1,1,1,1,48,1536]{6,5,4,3,2,1,0:T(8,128)(2,1)S(1)} %dynamic-slice_convert_fusion.12), channel_id=1, source_target_pairs={{0,4},{1,5},{2,6},{3,7},{4,0},{5,1},{6,2},{7,3},{8,12},{9,13},{10,... | collective-permute-start | bytes 442376 | tf_op jit(solution)/shard_map/ppermute | solution.py:635
  645.8 10.4 %collective-permute-start.13 = (bf16[1,1,1,1,1,48,2176]{6,5,4,3,2,1,0:T(8,128)(2,1)S(1)}, bf16[1,1,1,1,1,48,2176]{6,5,4,3,2,1,0:T(8,128)(2,1)S(1)}, u32[]{:S(2)}, u32[]{:S(2)}) collective-permute-start(bf16[1,1,1,1,1,48,2176]{6,5,4,3,2,1,0:T(8,128)(2,1)S(1)} %dynamic-slice_convert_fusion.11), channel_id=1, source_target_pairs={{0,4},{1,5},{2,6},{3,7},{4,0},{5,1},{6,2},{7,3},{8,12},{9,13},{10,... | collective-permute-start | bytes 626696 | tf_op jit(solution)/shard_map/ppermute | solution.py:635
  (81 other events, 857.5 us)

commit v3 on v2

--- a/solution.py
+++ b/solution.py
@@ -603,6 +603,543 @@
     )(table, rows_in, grad_in, weight_gate, weight_up, weight_down)
 
 
+def backward_kernel(
+    attn_gain_ref, ffn_gain_ref, cos_ref, sin_ref, seg_row_ref, seg_col_ref, lse_ref, key_ref,
+    value_ref, second0_ref, second1_ref, second2_ref, second3_ref, mixed_ref, cot_ref, att_ref,
+    query_ref, tok_ref, wo_ref, wq_ref, wk_ref, wv_ref, gg_ref, gu_ref, gd_ref, own_ref, sibling_ref,
+    query_out, kv_out, out_out, layer_ref, tokens_ref, gate_out, up_out, down_out, ra_ref, rb_ref, rf_ref,
+    pool, w_big, w_key, w_value, grad, proj, bias, key_acc, value_acc, gain_acc,
+    out_buf, out_land, query_buf, kv_buf, kv_land,
+    ex_land, ef_land, ec_land, ec_down_land, kept, stage, stage_down, load_sem, out_send, out_recv, ex_send, ex_recv, ef_send, ef_recv, ec_send, ec_recv,
+    halve_send, halve_recv, free_sem, store_sem,
+):
+    f32, bf16 = jnp.float32, jnp.bfloat16
+    grp, ep = lax.axis_index("grp"), lax.axis_index("ep")
+    core = lax.rem(grp, 2)
+    x = grp // 2
+    y = lax.rem(ep, 2)
+    z_low = lax.rem(ep // 2, 2)
+    z_high = ep // 4
+    by_y = (grp, ep + 1 - 2 * y)
+    by_z = (grp, ep + 2 - 4 * z_low)
+    by_far = (grp, ep + 4 - 8 * z_high)
+    by_core = (grp + 1 - 2 * core, ep)
+    by_x = (grp + 2 - 4 * x, ep)
+    first = (grp, by_y[1] * (1 - core) + by_z[1] * core)
+    second = (grp, by_z[1] * (1 - core) + by_y[1] * core)
+    rows, width = grad.shape
+    head = cos_ref.shape[1]
+    heads = width // head
+    key_width = key_ref.shape[1]
+    per_key = heads * head // key_width
+    block = width // 32
+
+    def remote(src, dst, send, recv, device):
+        return pltpu.make_async_remote_copy(
+            src_ref=src, dst_ref=dst, send_sem=send, recv_sem=recv, device_id=device,
+            device_id_type=pl.DeviceIdType.MESH,
+        )
+
+    partners = (by_core, by_y, by_z, by_x, by_far)
+    barrier = pltpu.get_barrier_semaphore()
+    for device in partners:
+        pl.semaphore_signal(barrier, inc=1, device_id=device, device_id_type=pl.DeviceIdType.MESH)
+    pl.semaphore_wait(barrier, 5)
+
+    wide_half = width // 2
+    quarter = width // 4
+    ex_dst = tuple(ex_land.at[m] for m in range(3))
+    ef_dst = tuple(ef_land.at[m] for m in range(3))
+    ec_dst = (ec_land.at[0], ec_land.at[1], ec_down_land)
+
+    def part(ref, m, index, size):
+        at = pl.ds(pl.multiple_of(index * size, size), size)
+        return ref.at[:, at] if m == 2 else ref.at[at, :]
+
+    grads = (gg_ref, gu_ref, gd_ref)
+
+    def ex_copy(m):
+        return remote(
+            part(grads[m], m, 1 - x, wide_half), ex_dst[m], ex_send.at[m], ex_recv.at[m], by_x
+        )
+
+    def ef_copy(m):
+        return remote(ex_dst[m], ef_dst[m], ef_send.at[m], ef_recv.at[m], by_far)
+
+    def ec_copy(m, base):
+        return remote(
+            part(base[m], m, 1 - core, quarter), ec_dst[m], ec_send.at[m], ec_recv.at[m], by_core
+        )
+
+    def kept_copy(m):
+        return pltpu.make_async_copy(part(grads[m], m, x, wide_half), kept, load_sem.at[20 + m])
+
+    def load(number, src, dst):
+        return pltpu.make_async_copy(src, dst, load_sem.at[number])
+
+    for m in range(3):
+        ex_copy(m).start()
+    loads = (
+        (own_ref.at[3], pool.at[6]),
+        (sibling_ref.at[3], pool.at[9]),
+        (own_ref.at[1], pool.at[5]),
+        (sibling_ref.at[1], pool.at[8]),
+        (second0_ref, pool.at[1]),
+        (second1_ref, pool.at[2]),
+        (second2_ref, pool.at[3]),
+        (second3_ref, pool.at[4]),
+        (mixed_ref, grad),
+        (cot_ref, pool.at[0]),
+        (wo_ref, w_big),
+        (own_ref.at[2], pool.at[7]),
+    )
+    for number, (src, dst) in enumerate(loads):
+        load(number, src, dst).start()
+
+    def wait_load(number):
+        load(number, *loads[number]).wait()
+
+    def add_into(dst, *others):
+        @pl.loop(0, rows // 128)
+        def _(step):
+            at = pl.ds(pl.multiple_of(step * 128, 128), 128)
+            total = dst[at, :].astype(f32)
+            for other in others:
+                total = total + other[at, :].astype(f32)
+            dst[at, :] = total.astype(bf16)
+
+    far_copy = lambda: remote(pool.at[6], rf_ref, out_send.at[0], out_recv.at[0], first)
+    first_copy = lambda: remote(pool.at[5], ra_ref, out_send.at[1], out_recv.at[1], first)
+    second_copy = lambda: remote(pool.at[7], rb_ref, out_send.at[2], out_recv.at[2], second)
+    wait_load(0)
+    wait_load(1)
+    add_into(pool.at[6], pool.at[9])
+    far_copy().start()
+    wait_load(2)
+    wait_load(3)
+    add_into(pool.at[5], pool.at[8])
+    first_copy().start()
+    sib2 = lambda: load(12, sibling_ref.at[2], pool.at[8])
+    sib2().start()
+    kept_copy(0).start()
+
+    for number in range(4, 10):
+        wait_load(number)
+    gain_acc[...] = jnp.zeros_like(gain_acc)
+
+    @pl.loop(0, rows // 128)
+    def _(step):
+        at = pl.ds(pl.multiple_of(step * 128, 128), 128)
+        value = grad[at, :]
+        scale = lax.rsqrt(jnp.mean(value * value, axis=-1, keepdims=True) + EPS)
+        normed = value * scale
+        down = (
+            pool[1, at, :].astype(f32)
+            + pool[2, at, :].astype(f32)
+            + pool[3, at, :].astype(f32)
+            + pool[4, at, :].astype(f32)
+        )
+        product = down * normed
+        gain_acc[1:2, :] += jnp.sum(product, axis=0, keepdims=True)
+        mean = jnp.mean(product * ffn_gain_ref[...], axis=-1, keepdims=True)
+        result = pool[0, at, :].astype(f32) + scale * (down * ffn_gain_ref[...] - normed * mean)
+        grad[at, :] = result
+        pool[3, at, :] = result.astype(bf16)
+
+    att_load = lambda: load(13, att_ref, pool.at[1])
+    query_load = lambda: load(14, query_ref, pool.at[2])
+    tok_load = lambda: load(15, tok_ref, pool.at[0])
+    key_weight_load = lambda: load(16, wk_ref, w_key)
+    value_weight_load = lambda: load(17, wv_ref, w_value)
+    for copy in (att_load, query_load, tok_load, key_weight_load, value_weight_load):
+        copy().start()
+
+    position = lax.broadcasted_iota(jnp.int32, (rows, rows), 0)
+    other_position = lax.broadcasted_iota(jnp.int32, (rows, rows), 1)
+    padding = seg_row_ref[...] == jnp.max(seg_row_ref[...])
+    allowed = (
+        (other_position <= position)
+        & (seg_col_ref[...] == seg_row_ref[...])
+        & (jnp.logical_not(padding) | (other_position == position))
+    )
+    bias[...] = jnp.where(allowed, 0.0, -1e30)
+
+    def dot_nt(a, b):
+        return lax.dot_general(a, b, (((1,), (1,)), ((), ())), preferred_element_type=f32)
+
+    def dot_tn(a, b):
+        return lax.dot_general(a, b, (((0,), (0,)), ((), ())), preferred_element_type=f32)
+
+    levels = ((core, by_core), (y, by_y), (x, by_x), (z_low, by_z), (z_high, by_far))
+    offsets = (0, 16, 24, 28, 30)
+    starts = [0]
+    for level, (bit, _) in enumerate(levels):
+        starts.append(starts[-1] + bit * (16 >> level))
+
+    def halve_copy(job, buf, land, level):
+        bit, device = levels[level]
+        size = 16 >> level
+        return remote(
+            buf.at[pl.ds(starts[level] + (1 - bit) * size, size)],
+            land.at[pl.ds(offsets[level], size)],
+            halve_send.at[job, level],
+            halve_recv.at[job, level],
+            device,
+        )
+
+    def absorb(job, buf, land, level, result=None):
+        halve_copy(job, buf, land, level).wait_recv()
+        size = 16 >> level
+        if result is None:
+
+            @pl.loop(0, size)
+            def _(i):
+                at = starts[level + 1] + i
+                buf[at] = (buf[at].astype(f32) + land[offsets[level] + i].astype(f32)).astype(bf16)
+
+        else:
+            result[...] = buf[starts[5]].astype(f32) + land[offsets[4]].astype(f32)
+        if job == 0:
+            pl.semaphore_signal(
+                free_sem.at[level], inc=1, device_id=levels[level][1],
+                device_id_type=pl.DeviceIdType.MESH,
+            )
+        if level < 4:
+            launch(job, level + 1)
+
+    jobs = ((out_buf, out_land), (query_buf, out_land), (kv_buf, kv_land))
+
+    def launch(job, level):
+        if job == 1:
+            pl.semaphore_wait(free_sem.at[level], 1)
+        halve_copy(job, *jobs[job], level).start()
+
+    def begin(job):
+        launch(job, 0)
+
+    def advance(job, level):
+        absorb(job, *jobs[job], level, (out_out, query_out, kv_out)[job] if level == 4 else None)
+
+    def place(buf, tile, value, columns):
+        for b in range(8):
+            high, low, odd = b >> 2, (b >> 1) & 1, b & 1
+            to = ((((tile & 1) * 2 + odd) * 2 + (tile >> 1)) * 2 + low) * 2 + high
+            buf[to, :, columns] = value[b * block : (b + 1) * block].astype(bf16)
+
+    att_load().wait()
+    for tile in range(4):
+        at = slice(tile * 8 * block, (tile + 1) * 8 * block)
+        place(out_buf, tile, dot_tn(pool[3, :, at], pool[1]), slice(None))
+    begin(0)
+    wait_load(10)
+    for half in range(2):
+        at = slice(half * rows // 2, (half + 1) * rows // 2)
+        pool[4, at, :] = dot_nt(pool[3, at, :], w_big[...]).astype(bf16)
+    query_weight_load = lambda: load(18, wq_ref, w_big)
+    query_weight_load().start()
+
+    tok_load().wait()
+
+    def first_norm(at):
+        value = pool[0, at, :].astype(f32)
+        scale = lax.rsqrt(jnp.mean(value * value, axis=-1, keepdims=True) + EPS)
+        return scale, value * scale
+
+    @pl.loop(0, rows // 128)
+    def _(step):
+        at = pl.ds(pl.multiple_of(step * 128, 128), 128)
+        pool[1, at, :] = (first_norm(at)[1] * attn_gain_ref[...]).astype(bf16)
+
+    def send_second():
+        wait_load(11)
+        sib2().wait()
+        far_copy().wait_recv()
+        far_load = load(19, rf_ref, pool.at[9])
+        far_load.start()
+        far_load.wait()
+        add_into(pool.at[7], pool.at[8], pool.at[9])
+        second_copy().start()
+
+    def expert_second(m):
+        kept_copy(m).wait()
+        ex_copy(m).wait_recv()
+        dst = ex_dst[m]
+        at_rows = dst.shape[0]
+
+        @pl.loop(0, at_rows // 128)
+        def _(step):
+            at = pl.ds(pl.multiple_of(step * 128, 128), 128)
+            dst[at, :] = (dst[at, :].astype(f32) + kept[at, :].astype(f32)).astype(bf16)
+
+        if m < 2:
+            kept_copy(m + 1).start()
+
+        @pl.when(core == 1)
+        def _():
+            ef_copy(m).start()
+
+        @pl.when(core == 0)
+        def _():
+            ec_copy(m, ex_dst).start()
+
+    results = (gate_out, up_out, down_out)
+
+    def store_copy(m):
+        return pltpu.make_async_copy(stage_down if m == 2 else stage, results[m], store_sem.at[m])
+
+    def expert_third(m):
+        @pl.when(core == 1)
+        def _():
+            ef_copy(m).wait_recv()
+            ec_copy(m, ef_dst).start()
+
+    def expert_last(m):
+        if m == 1:
+            store_copy(0).wait()
+        ec_copy(m, ex_dst).wait_recv()
+        at = pl.ds(pl.multiple_of(core * quarter, quarter), quarter)
+
+        def finish(base):
+            if m == 2:
+                stage_down[...] = base[:, at].astype(f32) + ec_dst[m][...].astype(f32)
+            else:
+                stage[...] = base[at, :].astype(f32) + ec_dst[m][...].astype(f32)
+
+        @pl.when(core == 0)
+        def _():
+            finish(ex_dst[m])
+
+        @pl.when(core == 1)
+        def _():
+            finish(ef_dst[m])
+
+        store_copy(m).start()
+
+    def turn_back(value, at):
+        swapped = pltpu.roll(value, head // 2, 1)
+        return value * cos_ref[at, :] - swapped * sin_ref[at, :]
+
+    scale = head ** (-0.5)
+    query_load().wait()
+    key_acc[...] = jnp.zeros_like(key_acc)
+    value_acc[...] = jnp.zeros_like(value_acc)
+
+    def between(number):
+        if number == 1:
+            advance(0, 0)
+        elif number == 3:
+            send_second()
+        elif number == 4:
+            expert_second(0)
+        elif number == 6:
+            advance(0, 1)
+        elif number == 9:
+            advance(0, 2)
+
+    for number in range(heads):
+        columns = slice(number * head, (number + 1) * head)
+        kv = number // per_key
+        kv_columns = slice(kv * head, (kv + 1) * head)
+        for half in range(2):
+            at = slice(half * rows // 2, (half + 1) * rows // 2)
+            seen = slice(0, (half + 1) * rows // 2)
+            q = pool[2, at, columns]
+            da = pool[4, at, columns]
+            k = key_ref[seen, kv_columns]
+            score = dot_nt(q, k) * scale + bias[at, seen]
+            probs = jnp.exp(score - lse_ref[at, number : number + 1])
+            dprob = dot_nt(da, value_ref[seen, kv_columns])
+            inner = jnp.sum(probs * dprob, axis=-1, keepdims=True)
+            dscore = (probs * (dprob - inner)).astype(bf16)
+            value_acc[seen, kv_columns] += dot_tn(probs.astype(bf16), da)
+            key_acc[seen, kv_columns] += dot_tn(dscore, q)
+            dq = jnp.dot(dscore, k, preferred_element_type=f32) * scale
+            proj[at, columns] = turn_back(dq, at).astype(bf16)
+        between(number)
+
+    for kv in range(key_width // head):
+        columns = slice(kv * head, (kv + 1) * head)
+        to = slice(width + kv * head, width + (kv + 1) * head)
+        proj[:, to] = turn_back(key_acc[:, columns] * scale, slice(None)).astype(bf16)
+        to = slice(width + key_width + kv * head, width + key_width + (kv + 1) * head)
+        proj[:, to] = value_acc[:, columns].astype(bf16)
+
+    for tile in range(4):
+        at = slice(tile * 8 * block, (tile + 1) * 8 * block)
+        place(query_buf, tile, dot_tn(pool[1, :, at], proj[:, :width]), slice(None))
+    begin(1)
+    for tile in range(4):
+        at = slice(tile * 8 * block, (tile + 1) * 8 * block)
+        place(kv_buf, tile, dot_tn(pool[1, :, at], proj[:, width:]), slice(0, 2 * key_width))
+    expert_second(1)
+    query_weight_load().wait()
+    key_weight_load().wait()
+    value_weight_load().wait()
+    for quarter_step in range(4):
+        at = slice(quarter_step * rows // 4, (quarter_step + 1) * rows // 4)
+        down = dot_nt(proj[at, :width], w_big[...])
+        down = down + dot_nt(proj[at, width : width + key_width], w_key[...])
+        down = down + dot_nt(proj[at, width + key_width :], w_value[...])
+        factor, normed = first_norm(at)
+        product = down * normed
+        gain_acc[0:1, :] += jnp.sum(product, axis=0, keepdims=True)
+        mean = jnp.mean(product * attn_gain_ref[...], axis=-1, keepdims=True)
+        grad[at, :] = grad[at, :] + factor * (down * attn_gain_ref[...] - normed * mean)
+        if quarter_step == 1:
+            advance(1, 0)
+    tokens_store = lambda: pltpu.make_async_copy(grad, tokens_ref, store_sem.at[3])
+    tokens_store().start()
+
+    gains = gain_acc[...]
+    high = gains.astype(bf16).astype(f32)
+    row = lax.broadcasted_iota(jnp.int32, gains.shape, 0)
+    lower = pltpu.roll(gains - high, 2, 0)
+    both = jnp.transpose(jnp.where(row < 2, high, lower))
+    both = jnp.concatenate([both, jnp.zeros((width, head - 8), f32)], axis=1)
+    for tile in range(4):
+        at = slice(tile * 8 * block, (tile + 1) * 8 * block)
+        place(kv_buf, tile, both[at], slice(2 * key_width, 2 * key_width + head))
+    begin(2)
+
+    expert_third(0)
+    expert_last(0)
+    advance(1, 1)
+    advance(2, 0)
+    advance(0, 3)
+    advance(2, 1)
+    expert_second(2)
+    advance(1, 2)
+    expert_third(1)
+    expert_last(1)
+    advance(2, 2)
+    advance(0, 4)
+    advance(1, 3)
+    advance(2, 3)
+
+    tokens_store().wait()
+    first_copy().wait_recv()
+    second_copy().wait_recv()
+    last_loads = (
+        (own_ref.at[0], pool.at[3]),
+        (sibling_ref.at[0], pool.at[4]),
+        (ra_ref, pool.at[8]),
+        (rb_ref, pool.at[9]),
+        (mixed_ref, grad),
+    )
+    for number, (src, dst) in enumerate(last_loads):
+        load(number, src, dst).start()
+    for number, (src, dst) in enumerate(last_loads):
+        load(number, src, dst).wait()
+
+    @pl.loop(0, rows // 128)
+    def _(step):
+        at = pl.ds(pl.multiple_of(step * 128, 128), 128)
+        total = grad[at, :]
+        for i in (3, 4, 8, 9):
+            total = total + pool[i, at, :].astype(f32)
+        pool[3, at, :] = total.astype(bf16)
+
+    layer_store = pltpu.make_async_copy(pool.at[3], layer_ref, store_sem.at[4])
+    layer_store.start()
+    advance(1, 4)
+    advance(2, 4)
+    expert_third(2)
+    expert_last(2)
+
+    for copy in (far_copy, first_copy, second_copy):
+        copy().wait_send()
+    for m in range(3):
+        ex_copy(m).wait_send()
+        ec_copy(m, ex_dst).wait_send()
+
+        @pl.when(core == 1)
+        def _(m=m):
+            ef_copy(m).wait_send()
+
+        if m > 0:
+            store_copy(m).wait()
+    for job in range(3):
+        for level in range(5):
+            halve_copy(job, *jobs[job], level).wait_send()
+    layer_store.wait()
+
+
+def backward_call(vmem_args, any_args):
+    f32, bf16 = jnp.float32, jnp.bfloat16
+    rows, head = vmem_args[2].shape
+    key_width = vmem_args[7].shape[1]
+    width = vmem_args[0].shape[1]
+    hidden = any_args[13].shape[1]
+    block = width // 32
+    extra = 2 * key_width + head
+    anywhere = pl.BlockSpec(memory_space=pl.ANY)
+    inside = pl.BlockSpec(memory_space=pltpu.VMEM)
+    shape = jax.ShapeDtypeStruct
+    dma = pltpu.SemaphoreType.DMA
+    vmem = pltpu.VMEM
+    return pl.pallas_call(
+        backward_kernel,
+        out_shape=(
+            shape((block, width), f32),
+            shape((block, extra), f32),
+            shape((block, width), f32),
+            shape((rows, width), bf16),
+            shape((rows, width), f32),
+            shape((width // 4, hidden), f32),
+            shape((width // 4, hidden), f32),
+            shape((hidden, width // 4), f32),
+            shape((rows, width), bf16),
+            shape((rows, width), bf16),
+            shape((rows, width), bf16),
+        ),
+        in_specs=[inside] * len(vmem_args) + [anywhere] * len(any_args),
+        out_specs=(inside,) * 3 + (anywhere,) * 8,
+        scratch_shapes=[
+            vmem((10, rows, width), bf16),
+            vmem((width, width), bf16),
+            vmem((width, key_width), bf16),
+            vmem((width, key_width), bf16),
+            vmem((rows, width), f32),
+            vmem((rows, width + 2 * key_width), bf16),
+            vmem((rows, rows), f32),
+            vmem((rows, key_width), f32),
+            vmem((rows, key_width), f32),
+            vmem((8, width), f32),
+            vmem((32, block, width), bf16),
+            vmem((31, block, width), bf16),
+            vmem((32, block, width), bf16),
+            vmem((32, block, extra), bf16),
+            vmem((31, block, extra), bf16),
+            vmem((3, width // 2, hidden), bf16),
+            vmem((3, width // 2, hidden), bf16),
+            vmem((2, width // 4, hidden), bf16),
+            vmem((hidden, width // 4), bf16),
+            vmem((width // 2, hidden), bf16),
+            vmem((width // 4, hidden), f32),
+            vmem((hidden, width // 4), f32),
+            dma((23,)),
+            dma((3,)),
+            dma((3,)),
+            dma((3,)),
+            dma((3,)),
+            dma((3,)),
+            dma((3,)),
+            dma((3,)),
+            dma((3,)),
+            dma((3, 5)),
+            dma((3, 5)),
+            pltpu.SemaphoreType.REGULAR((5,)),
+            dma((5,)),
+        ],
+        compiler_params=pltpu.CompilerParams(
+            collective_id=1, has_side_effects=True, vmem_limit_bytes=64 * 2**20
+        ),
+        cost_estimate=pl.CostEstimate(
+            flops=30 * rows * width * width, bytes_accessed=60 * 2**20, transcendentals=0
+        ),
+    )(*vmem_args, *any_args)
+
+
 def local_dense(
     tokens,
     segment_ids,
@@ -631,25 +1168,8 @@
     side = (me // bit_x) % 2
     on_core1 = core == 1
 
-    def swap(value, mask):
-        return lax.ppermute(value, names, [(i, i ^ mask) for i in range(count)])
-
-    def swap_mixed(value, mask0, mask1):
-        return lax.ppermute(
-            value, names, [(i, i ^ (mask1 if i & bit_core else mask0)) for i in range(count)]
-        )
-
     def swap_core1(value, mask):
         return lax.ppermute(value, names, [(i, i ^ mask) for i in range(count) if i & bit_core])
-
-    def reduce_outputs(own_parts, sibling_parts):
-        own, to_first, to_second, far = [
-            own_parts[i].astype(f32) + sibling_parts[i].astype(f32) for i in range(4)
-        ]
-        to_second = to_second + swap_mixed(far.astype(bf16), bit_y, bit_z).astype(f32)
-        return own + swap_mixed(to_first.astype(bf16), bit_y, bit_z).astype(f32) + swap_mixed(
-            to_second.astype(bf16), bit_z, bit_y
-        ).astype(f32)
 
     def fetch(weight):
         rows = weight.shape[0] // 2
@@ -659,31 +1179,6 @@
         low = jnp.where(side == 0, here, there)
         high = jnp.where(side == 0, there, here)
         return jnp.where(on_core1, jnp.concatenate([low, high], axis=0), weight)
-
-    def give(grad, dim):
-        size = grad.shape[dim] // 2
-        sent = lax.dynamic_slice_in_dim(grad, (1 - side) * size, size, dim).astype(bf16)
-        kept = lax.dynamic_slice_in_dim(grad, side * size, size, dim)
-        half = kept.astype(f32) + swap(sent, bit_x).astype(f32)
-        foreign = swap_core1(half.astype(bf16), bit_far).astype(f32)
-        base = jnp.where(on_core1, foreign, half)
-        size = size // 2
-        sent = lax.dynamic_slice_in_dim(base, (1 - core) * size, size, dim).astype(bf16)
-        kept = lax.dynamic_slice_in_dim(base, core * size, size, dim)
-        return kept + swap(sent, bit_core).astype(f32)
-
-    def reduce_all(value):
-        order = [bit_core, bit_x, bit_y, bit_z, bit_far]
-        bits = [bit_x, bit_core, bit_far, bit_z, bit_y]
-        rows, columns = value.shape
-        block = value.reshape((2,) * 5 + (rows // count, columns))
-        for mask in order:
-            axis = bits.index(mask)
-            mine = (me // mask) % 2
-            sent = lax.dynamic_slice_in_dim(block, 1 - mine, 1, axis)
-            kept = lax.dynamic_slice_in_dim(block, mine, 1, axis)
-            block = kept.astype(f32) + swap(sent.astype(bf16), mask).astype(f32)
-        return block.reshape(rows // count, columns)
 
     weight_gate = fetch(expert_gate[0])
     weight_up = fetch(expert_up[0])
@@ -756,92 +1251,67 @@
         out_sib,
         *second_parts,
     ) = moe_call(table.T, h_second, cotangent, weight_gate, weight_up, weight_down)
-    second_grad = sum(part.astype(f32) for part in second_parts)
-    expert_sums = (give(gate_part, 0)[None], give(up_part, 0)[None], give(down_part, 1)[None])
-    layer_out = (mixed + reduce_outputs(out_own, out_sib)).astype(bf16)
-    grad_out = cotangent.astype(f32)
-    ffn_gain_part = jnp.sum(second_grad * normed_second, axis=0)
-    normed_grad = second_grad * ffn_gain
-    mixed_grad = grad_out + scale_second * (
-        normed_grad - normed_second * jnp.mean(normed_grad * normed_second, axis=-1, keepdims=True)
-    )
-    mixed_low = mixed_grad.astype(jnp.bfloat16)
-    output_part = jnp.einsum("ti,td->di", attended, mixed_low, preferred_element_type=jnp.float32)
-    output_grad = reduce_all(output_part).T
-    attended_grad = jnp.einsum(
-        "td,id->ti", mixed_low, output_weight, preferred_element_type=jnp.float32
-    )
-    attended_grad = attended_grad.astype(jnp.bfloat16).reshape(
-        length_total, key_heads, q_per_kv, HEAD_SIZE
-    )
-    probs = jnp.exp(scores_of(query_rot, key_rot, allowed) - log_total)
-    probs_again = probs.astype(jnp.bfloat16)
-    value_part_grad = jnp.einsum(
-        "kgts,tkgd->skd", probs_again, attended_grad, preferred_element_type=jnp.float32
-    )
-    prob_grad = jnp.einsum(
-        "tkgd,skd->kgts", attended_grad, value_low, preferred_element_type=jnp.float32
-    )
-    inner = jnp.sum(probs * prob_grad, axis=-1, keepdims=True)
-    score_grad = (probs * (prob_grad - inner)).astype(jnp.bfloat16)
-    qrot_grad = jnp.einsum(
-        "kgts,skd->tkgd", score_grad, key_rot, preferred_element_type=jnp.float32
-    ) * HEAD_SIZE ** (-0.5)
-    krot_grad = jnp.einsum(
-        "kgts,tkgd->skd", score_grad, query_rot, preferred_element_type=jnp.float32
-    ) * HEAD_SIZE ** (-0.5)
-    query_grad_low = unrotate(
-        qrot_grad.reshape(length_total, query_heads, HEAD_SIZE), cosine_table, sine_table
-    )
-    query_grad_low = query_grad_low.astype(jnp.bfloat16).reshape(
-        length_total, query_heads * HEAD_SIZE
-    )
-    key_grad_low = (
-        unrotate(krot_grad, cosine_table, sine_table)
-        .astype(jnp.bfloat16)
-        .reshape(length_total, key_heads * HEAD_SIZE)
-    )
-    value_grad_low = value_part_grad.astype(jnp.bfloat16).reshape(
-        length_total, key_heads * HEAD_SIZE
-    )
-    projected = jnp.concatenate([query_grad_low, key_grad_low, value_grad_low], axis=1)
-    projected_part = jnp.einsum("td,ti->di", h_first, projected, preferred_element_type=f32)
-    first_grad = jnp.einsum(
-        "ti,di->td", query_grad_low, query_weight, preferred_element_type=jnp.float32
-    )
-    first_grad = first_grad + jnp.einsum(
-        "ti,di->td", key_grad_low, key_matrix, preferred_element_type=jnp.float32
-    )
-    first_grad = first_grad + jnp.einsum(
-        "ti,di->td", value_grad_low, value_matrix, preferred_element_type=jnp.float32
-    )
-    attn_gain_part = jnp.sum(first_grad * normed_first, axis=0)
-    normed_first_grad = first_grad * attn_gain
-    tokens_grad = mixed_grad + scale_first * (
-        normed_first_grad
-        - normed_first * jnp.mean(normed_first_grad * normed_first, axis=-1, keepdims=True)
-    )
-    gains = jnp.stack([attn_gain_part, ffn_gain_part], axis=1)
-    gains_high = gains.astype(bf16).astype(f32)
-    gains = jnp.concatenate([gains_high, gains - gains_high], axis=1)
-    gains = jnp.pad(gains, ((0, 0), (0, 124)))
-    shared = reduce_all(jnp.concatenate([projected_part, gains], axis=1))
-    split_q = query_weight.shape[1]
-    split_k = split_q + key_matrix.shape[1]
+    log_total = log_total.reshape(query_heads, length_total).T
+    log_total = jnp.pad(log_total, ((0, 0), (0, HEAD_SIZE - query_heads)))
+    cosine = cosine_table[:, 0, :]
+    sine = sine_table[:, 0, :]
+    (
+        query_grad,
+        extra_grad,
+        output_grad,
+        layer_out,
+        tokens_grad,
+        gate_grad,
+        up_grad,
+        down_grad,
+        _,
+        _,
+        _,
+    ) = backward_call(
+        (
+            attn_gain[None, :],
+            ffn_gain[None, :],
+            jnp.concatenate([cosine, cosine], axis=1),
+            jnp.concatenate([-sine, sine], axis=1),
+            segment_ids,
+            segment_ids.T,
+            log_total,
+            key_rot.reshape(length_total, -1),
+            value_low.reshape(length_total, -1),
+        ),
+        (
+            *second_parts,
+            mixed,
+            cotangent,
+            attended,
+            query_rot.reshape(length_total, -1),
+            tokens,
+            output_weight,
+            query_weight,
+            key_matrix,
+            value_matrix,
+            gate_part,
+            up_part,
+            down_part,
+            out_own,
+            out_sib,
+        ),
+    )
+    split_k = key_matrix.shape[1]
     split_v = split_k + value_matrix.shape[1]
-    gain_sums = shared[:, split_v : split_v + 2] + shared[:, split_v + 2 : split_v + 4]
+    gain_sums = extra_grad[:, split_v : split_v + 2] + extra_grad[:, split_v + 2 : split_v + 4]
     return (
         layer_out,
         tokens_grad,
-        shared[:, :split_q],
-        shared[:, split_q:split_k],
-        shared[:, split_k:split_v],
-        output_grad,
+        query_grad,
+        extra_grad[:, :split_k],
+        extra_grad[:, split_k:split_v],
+        output_grad.T,
         gain_sums[:, 0],
         gain_sums[:, 1],
-        expert_sums[0],
-        expert_sums[1],
-        expert_sums[2],
+        gate_grad[None],
+        up_grad[None],
+        down_grad[None],
     )
 
 

time: 663 us -> 512 us (0.77)
  Pallas kernels: 242 us -> 417 us
  waiting for transfers between devices: 128 us -> 0.02 us
  other arithmetic: 97.5 us -> 26.8 us
  starting transfers between devices: 66.4 us -> 8.46 us
  matrix products: 69.2 us -> 22.5 us
  local copies, waits for them, and re-layouts: 53.1 us -> 32.7 us
    pallas_call x0 -> x1, Pallas kernels: none -> 181 us  [backward_call(): pl.pallas_call(backward_kernel, out_shape=(shape((block, width), f32), sh...]
    ppermute x19 -> x0, waiting for transfers between devices: 128 us -> none  [the longest x16 83.5 us: swap(): return lax.ppermute(value, names, [(i, i ^ mask) for i in range(count)])]
    ppermute x19 -> x0, starting transfers between devices: 53.4 us -> none  [the longest x16 50.3 us: swap(): return lax.ppermute(value, names, [(i, i ^ mask) for i in range(count)])]
    dot_general x10 -> x0, matrix products: 47.9 us -> none  [the longest x1 9.69 us: local_dense(): jnp.einsum('tkgd,skd->kgts', attended_grad, value_low, preferred_element_...]
    convert_element_type x7 -> x1, other arithmetic: 23.8 us -> 0.85 us  [local_dense(): apply_rotary(key_rows, cosine_table, sine_table).astype(jnp.bfloat16)]
    add x10 -> x1, other arithmetic: 11.6 us -> 0.98 us  [local_dense(): extra_grad[:, split_v:split_v + 2] + extra_grad[:, split_v + 2:split_v + 4]]
    concatenate x4 -> x2, other arithmetic: 11 us -> 1.1 us  [the longest x1 0.99 us: local_dense(): jnp.concatenate([cosine, cosine], axis=1)]
    convert_element_type x14 -> x2, local copies, waits for them, and re-layouts: 13 us -> 4.17 us  [the longest x1 2.6 us: local_dense(): attended.reshape(length_total, query_heads * HEAD_SIZE).astype(jnp.bfloat16)]
  transfers between devices with their start and end apart: 28 -> 6, of which waited for: 8 -> 0; matrix products, arithmetic and copies ran while one was open for 29% -> 12% of each run, Pallas kernels for 0% -> 0%
where the time goes in v3:
time: 512 us; the launch traced here: 508 us
  Pallas kernels  417 us (81%)
  local copies, waits for them, and re-layouts  32.7 us (6%)
  other arithmetic  26.8 us (5%)
  matrix products  22.5 us (4%)
  starting transfers between devices  8.46 us (2%)
    pallas_call x1, Pallas kernels, moe_call(): pl.pallas_call(moe_kernel, out_shape=(wide, wide, tall, four, four, chunk...  235 us
    pallas_call x1, Pallas kernels, backward_call(): pl.pallas_call(backward_kernel, out_shape=(shape((block, width), f32), sh...  181 us
    unnamed x71, local copies, waits for them, and re-layouts  14 us
  transfers between devices with their start and end apart: 6, of which 0 were waited for; matrix products, arithmetic and copies ran while one was open for 12% of the time, Pallas kernels for 0%

profile of v3, /device:TPU:0, one launch (start us, length us, event | category | flops | bytes accessed | tf_op | source)
XLA Modules:
  0.0 508.4 jit_solution(6327870195621455012)
XLA Ops:
  0.7 2.5 dynamic-slice_bitcast_fusion.1
  3.2 1.8 collective-permute-start.2
  5.0 2.4 dynamic-slice_bitcast_fusion.2
  7.4 1.8 collective-permute-start
  9.2 1.1 dynamic-slice_bitcast_fusion
  10.3 1.7 collective-permute-start.4
  13.3 1.8 fusion.3
  15.1 2.4 convolution_convert_fusion.value_ref
  21.2 1.8 fusion.17
  23.3 4.7 fusion.22
  29.5 1.5 copy.61
  31.3 1.6 multiply_subtract_fusion
  32.9 3.4 fusion.1
  36.4 2.6 fusion
  39.1 4.3 fusion.6
  46.0 6.9 %multiply_reduce_fusion = (f32[512]{0:T(512)S(1)}, f32[512,1536]{1,0:T(8,128)}) fusion(bf16[512,1536]{0,1:T(8,128)(2,1)S(1)} %bitcast.66, bf16[1536,1536]{1,0:T(8,128)(2,1)} %wo_ref.1, bf16[512,1536]{1,0:T(8,128)(2,1)S(1)} %copy-done.15), kind=kOutput, calls=%fused_computation.13 | convolution fusion | flops 2419064320 | bytes 11012096 | tf_op jit(solution)/shard_map/dot_general | solution.py:1241
  54.6 1.7 collective-permute-start.5
  57.5 2.6 copy.68.att_ref
  61.6 1.6 copy.69.query_ref
  64.0 3.4 multiply_convert_fusion.h_ref
  68.1 1.4 broadcast_select_fusion.3
  69.6 1.9 broadcast_select_fusion.1
  72.0 2.1 maximum_select_fusion.2.wd_ref
  74.0 1.6 broadcast_select_fusion.5
  76.8 2.9 maximum_select_fusion
  79.6 235.2 %shard_map.221 = (bf16[1536,768]{1,0:T(8,128)(2,1)}, bf16[1536,768]{1,0:T(8,128)(2,1)}, bf16[768,1536]{1,0:T(8,128)(2,1)}, bf16[4,512,1536]{2,1,0:T(8,128)(2,1)}...) custom-call(f32[8,512]{1,0:T(8,128)} %bitcast.77, ...), custom_call_target="tpu_custom_call" | custom-call | flops 86973087744 | bytes 62914560 | tf_op jit(solution)/shard_map/pallas_call | solution.py:564
  314.9 181.3 %shard_map.222 = (f32[48,1536]{1,0:T(8,128)}, f32[48,640]{1,0:T(8,128)}, f32[48,1536]{1,0:T(8,128)}, bf16[512,1536]{1,0:T(8,128)(2,1)}, f32[512,1536]{1,0:T(8,12...) custom-call(f32[1,1536]{1,0:T(1,128)} %broadcast_in_dim.30.attn_gain, ...), custom_call_target="tpu_custom_call" | custom-call | flops 36238786560 | bytes 62914560 | tf_op jit(solution)/shard_map/pallas_call | solution.py:1080
  497.2 1.5 fusion.27
  499.3 2.7 copy.87
  502.0 1.7 copy.88
  505.1 1.0 copy.91
  506.1 1.0 copy.92
  (101 shorter events, 21.2 us)
Async XLA Ops:
  0.7 8.5 %copy-start.1 = (bf16[1,768,1536]{2,1,0:T(8,128)(2,1)S(1)}, bf16[1,768,1536]{2,1,0:T(8,128)(2,1)}, u32[]{:S(2)}) copy-start(bf16[1,768,1536]{2,1,0:T(8,128)(2,1)} %param.26) | copy-start | bytes 7077892
  3.2 8.8 %copy-start.25 = (s32[1,512]{1,0:T(1,128)S(1)}, s32[1,512]{1,0:T(1,128)}, u32[]{:S(2)}) copy-start(s32[1,512]{1,0:T(1,128)} %seg_row_ref.1) | copy-start | bytes 6148
  3.2 49.8 %collective-permute-start.2 = (bf16[768,768]{1,0:T(8,128)(2,1)}, bf16[768,768]{1,0:T(8,128)(2,1)}, u32[]{:S(2)}, u32[]{:S(2)}) collective-permute-start(bf16[768,768]{1,0:T(8,128)(2,1)} %dynamic-slice_bitcast_fusion.1), channel_id=1, source_target_pairs={{8,12},{9,13},{10,14},{11,15},{12,8},{13,9},{14,10},{15,11},{24,28... | collective-permute-start | bytes 3538952 | tf_op jit(solution)/shard_map/ppermute | solution.py:1172
  7.4 7.7 %copy-start.27 = (f32[1536]{0:T(1024)S(1)}, f32[1536]{0:T(1024)}, u32[]{:S(2)}) copy-start(f32[1536]{0:T(1024)} %param.18) | copy-start | bytes 18436
  7.4 60.0 %collective-permute-start = (bf16[768,768]{1,0:T(8,128)(2,1)}, bf16[768,768]{1,0:T(8,128)(2,1)}, u32[]{:S(2)}, u32[]{:S(2)}) collective-permute-start(bf16[768,768]{1,0:T(8,128)(2,1)} %dynamic-slice_bitcast_fusion.2), channel_id=1, source_target_pairs={{8,12},{9,13},{10,14},{11,15},{12,8},{13,9},{14,10},{15,11},{24,28... | collective-permute-start | bytes 3538952 | tf_op jit(solution)/shard_map/ppermute | solution.py:1172
  10.3 44.3 %collective-permute-start.4 = (bf16[384,1536]{1,0:T(8,128)(2,1)}, bf16[384,1536]{1,0:T(8,128)(2,1)}, u32[]{:S(2)}, u32[]{:S(2)}) collective-permute-start(bf16[384,1536]{1,0:T(8,128)(2,1)} %dynamic-slice_bitcast_fusion), channel_id=1, source_target_pairs={{8,12},{9,13},{10,14},{11,15},{12,8},{13,9},{14,10},{15,11},{24,28... | collective-permute-start | bytes 3538952 | tf_op jit(solution)/shard_map/ppermute | solution.py:1172
  15.1 3.3 copy-start.14
  15.1 3.3 copy-start.30
  23.1 5.0 copy-start.5
  23.1 5.0 copy-start.7
  31.0 1.9 copy-start
  32.9 3.5 copy-start.10
  32.9 3.5 copy-start.12
  36.4 2.7 copy-start.24
  43.3 9.6 %copy-start.16 = (bf16[2,128,6,512]{3,1,2,0:T(8,128)(2,1)}, bf16[2,128,6,512]{3,1,2,0:T(8,128)(2,1)S(1)}, u32[]{:S(2)}) copy-start(bf16[2,128,6,512]{3,1,2,0:T(8,128)(2,1)S(1)} %fusion.6) | copy-start | bytes 4718596
  43.4 2.6 copy-start.15
  46.0 7.7 %copy-start.11 = (bf16[512,2,64]{2,0,1:T(8,128)(2,1)S(1)}, bf16[512,2,64]{2,0,1:T(8,128)(2,1)}, u32[]{:S(2)}) copy-start(bf16[512,2,64]{2,0,1:T(8,128)(2,1)} %copy-done.10) | copy-start | bytes 393220
  46.0 7.7 %copy-start.13 = (bf16[512,2,64]{2,0,1:T(8,128)(2,1)S(1)}, bf16[512,2,64]{2,0,1:T(8,128)(2,1)}, u32[]{:S(2)}) copy-start(bf16[512,2,64]{2,0,1:T(8,128)(2,1)} %copy-done.12) | copy-start | bytes 393220
  46.0 10.3 %copy-start.28 = (f32[512,4]{0,1:T(4,128)S(1)}, f32[512,4]{0,1:T(4,128)}, u32[]{:S(2)}) copy-start(f32[512,4]{0,1:T(4,128)} %param.17) | copy-start | bytes 24580
  46.0 10.3 %copy-start.29 = (s32[512,4]{0,1:T(4,128)S(1)}, s32[512,4]{0,1:T(4,128)}, u32[]{:S(2)}) copy-start(s32[512,4]{0,1:T(4,128)} %param.16) | copy-start | bytes 24580
  53.0 7.2 %copy-start.26 = (f32[1536]{0:T(1024)S(1)}, f32[1536]{0:T(1024)}, u32[]{:S(2)}) copy-start(f32[1536]{0:T(1024)} %param.19) | copy-start | bytes 18436
  53.0 15.2 %collective-permute-start.3 = (bf16[768,768]{1,0:T(8,128)(2,1)}, bf16[768,768]{1,0:T(8,128)(2,1)S(1)}, u32[]{:S(2)}, u32[]{:S(2)}) collective-permute-start(bf16[768,768]{1,0:T(8,128)(2,1)} %collective-permute-done.2), channel_id=1, source_target_pairs={{8,24},{9,25},{10,26},{11,27},{12,28},{13,29},{14,30},{15,31},{24,... | collective-permute-start | bytes 3538952 | tf_op jit(solution)/shard_map/ppermute | solution.py:1172
  54.6 15.0 %collective-permute-start.5 = (bf16[384,1536]{1,0:T(8,128)(2,1)}, bf16[384,1536]{1,0:T(8,128)(2,1)}, u32[]{:S(2)}, u32[]{:S(2)}) collective-permute-start(bf16[384,1536]{1,0:T(8,128)(2,1)} %collective-permute-done.4), channel_id=1, source_target_pairs={{8,24},{9,25},{10,26},{11,27},{12,28},{13,29},{14,30},{15,31},{24,... | collective-permute-start | bytes 3538952 | tf_op jit(solution)/shard_map/ppermute | solution.py:1172
  67.4 6.6 %collective-permute-start.1 = (bf16[768,768]{1,0:T(8,128)(2,1)}, bf16[768,768]{1,0:T(8,128)(2,1)S(1)}, u32[]{:S(2)}, u32[]{:S(2)}) collective-permute-start(bf16[768,768]{1,0:T(8,128)(2,1)} %collective-permute-done), channel_id=1, source_target_pairs={{8,24},{9,25},{10,26},{11,27},{12,28},{13,29},{14,30},{15,31},{24,... | collective-permute-start | bytes 3538952 | tf_op jit(solution)/shard_map/ppermute | solution.py:1172
  69.6 2.4 copy-start.2
  74.0 2.0 copy-start.3
  74.0 2.7 copy-start.4
  496.2 5.8 %copy-start.9 = (f32[512,1536]{1,0:T(8,128)S(1)}, f32[512,1536]{1,0:T(8,128)}, u32[]{:S(2)}) copy-start(f32[512,1536]{1,0:T(8,128)} %get-tuple-element.84) | copy-start | bytes 9437188
  502.0 2.4 copy-start.21
  502.0 3.1 copy-start.19
  503.7 2.5 copy-start.18
  505.1 2.0 copy-start.17
  (5 other events, 7.5 us)
